TPU v7x, 256 devices: a whole 4x4x8 slice. The times are simulated.
256 devices in a mesh: grp: 2 (over core), seq: 16 (over x, y), row: 8 (over z).
Axes of the slice: x: 4, y: 4, z: 8, core: 2. Of those that a mesh axis runs over, the one named last changes fastest.
Arguments:
- latent_pool: bfloat16 [2, 2048, 64, 576], P('grp', ('seq', 'row')), may hold values from -24 to 24
- block_table: int32 [2, 128, 16, 1], P('grp', ('seq', 'row')), may hold values from 0 to 15, as said below
- lengths: int32 [2, 16], replicated, may hold values from 1024 to 8192
- row_request: int32 [2, 16], P('grp'), may hold values from 0 to 15, each once within a row
- queries: bfloat16 [2, 16, 4, 128, 192], P('grp', 'row', None, 'seq'), may hold values from -24 to 24
- new_latent: bfloat16 [2, 16, 4, 576], P('grp', 'row'), may hold values from -6 to 6
- w_uk: bfloat16 [128, 128, 512], P('seq'), may hold values from -0.5 to 0.5
- w_uv: bfloat16 [128, 512, 128], P('seq'), may hold values from -0.25 to 0.25
Outputs:
- attn_out: bfloat16 [2, 16, 4, 128, 128], P('grp', 'row', None, 'seq')
Inputs may be any that keep to these rules, and one draw needn't show every extreme that they name: Each block block_table[g, d] holds every page number of 0 to 15 once. row_request[g] is a permutation of the 16 requests.
All inputs are finite; a program needn't handle non-finite values.
Results may differ from a plain program's by a relative error of at most 0.02.
Values may be sent and summed in bfloat16 or wider, within the bound.
No kernel may reach another device: no remote copies, remote signals or barrier semaphores. Data moves between devices by JAX's collectives and lax.ppermute only.
A program may use at most 64 MiB of HBM per device.

v0:
```python
import jax
import jax.numpy as jnp
from jax import lax
from jax.sharding import PartitionSpec as P

FILL_LOW = -1e30


def from_partner(block, axis, stride):
    count = lax.axis_size(axis)
    route = []
    for low in range(count):
        high = low | 1 << stride
        if high != low and high < count:
            route += [(low, high), (high, low)]
    return lax.ppermute(block, axis, route)


def per_device(latent_pool, block_table, lengths, row_request, queries, new_latent, w_uk, w_uv):
    n_seq = lax.axis_size("seq")
    n_row = lax.axis_size("row")
    seq_index = lax.axis_index("seq")
    row_index = lax.axis_index("row")
    nope_dim = w_uk.shape[1]
    latent_dim = w_uk.shape[2]
    head_dev = w_uk.shape[0]
    score_scale = queries.shape[4] ** (-0.5)
    gathered = latent_pool[0][block_table[0, 0]]
    n_reqs, blocks_dev, page_rows, lat_width = gathered.shape
    block_len = blocks_dev * page_rows
    local_cache = gathered.reshape(n_reqs, block_len, lat_width)
    partner = from_partner(local_cache, "grp", 0)
    ordered = partner[row_request[0]]
    rows_dev = n_reqs // n_row
    piece_len = block_len // n_seq
    pieces = ordered.reshape(n_reqs, n_seq, piece_len, lat_width).transpose(1, 0, 2, 3)
    slot_ids = jnp.arange(n_seq * n_row * piece_len, dtype=jnp.int32)
    source_slot = slot_ids // piece_len
    offset_in = slot_ids % piece_len
    decode_cache = lax.all_to_all(
        pieces.reshape(n_seq * n_reqs, piece_len, lat_width),
        ("seq", "row"),
        split_axis=0,
        concat_axis=1,
        tiled=True,
    )
    positions = source_slot * block_len + seq_index * piece_len + offset_in
    batch_len = lax.dynamic_index_in_dim(lengths, 1 - lax.axis_index("grp"), 0, keepdims=False)
    my_rows = lax.dynamic_slice_in_dim(row_request[0], row_index * rows_dev, rows_dev)
    row_len = batch_len[my_rows]
    in_prompt = (positions[None, :] < row_len[:, None])[:, None, None, :]
    query_raw = queries[0]
    q_lat = jnp.einsum(
        "rnhk,hkc->rnhc", query_raw[..., :nope_dim], w_uk, preferred_element_type=jnp.float32
    ).astype(jnp.bfloat16)
    own_query = jnp.concatenate([q_lat, query_raw[..., nope_dim:]], axis=-1)
    all_queries = lax.all_gather(own_query, "seq", axis=2, tiled=True)
    scores = (
        jnp.einsum("rnhc,rpc->rnhp", all_queries, decode_cache, preferred_element_type=jnp.float32)
        * score_scale
    )
    best_score = jnp.max(jnp.where(in_prompt, scores, FILL_LOW), axis=-1)
    weights = jnp.where(in_prompt, jnp.exp(scores - best_score[..., None]), 0.0)
    weight_sum = jnp.sum(weights, axis=-1)
    value_sum = jnp.einsum(
        "rnhp,rpc->rnhc",
        weights.astype(jnp.bfloat16),
        decode_cache[..., :latent_dim],
        preferred_element_type=jnp.float32,
    )
    lead_shape = best_score.shape[:2]
    got_best, got_sum, got_value = (
        lax.all_to_all(best_score, "seq", split_axis=2, concat_axis=2, tiled=True),
        lax.all_to_all(weight_sum, "seq", split_axis=2, concat_axis=2, tiled=True),
        lax.all_to_all(value_sum, "seq", split_axis=2, concat_axis=2, tiled=True),
    )
    got_best = got_best.reshape(lead_shape + (n_seq, head_dev))
    got_sum = got_sum.reshape(lead_shape + (n_seq, head_dev))
    got_value = got_value.reshape(lead_shape + (n_seq, head_dev, latent_dim))
    best_own = jnp.max(got_best, axis=2)
    factor = jnp.exp(got_best - best_own[:, :, None, :])
    sum_own = jnp.sum(got_sum * factor, axis=2)
    value_own = jnp.sum(got_value * factor[..., None], axis=2)
    new_keys = new_latent[0]
    new_scores = (
        jnp.einsum("rnhc,rjc->rnhj", own_query, new_keys, preferred_element_type=jnp.float32)
        * score_scale
    )
    new_steps = jnp.arange(new_keys.shape[1], dtype=jnp.int32)
    causal_ok = (new_steps[None, :] <= new_steps[:, None])[None, :, None, :]
    new_best = jnp.max(jnp.where(causal_ok, new_scores, FILL_LOW), axis=-1)
    final_best = jnp.maximum(best_own, new_best)
    rescale = jnp.exp(best_own - final_best)
    new_weights = jnp.where(causal_ok, jnp.exp(new_scores - final_best[..., None]), 0.0)
    final_sum = sum_own * rescale + jnp.sum(new_weights, axis=-1)
    final_value = value_own * rescale[..., None] + jnp.einsum(
        "rnhj,rjc->rnhc",
        new_weights.astype(jnp.bfloat16),
        new_keys[..., :latent_dim],
        preferred_element_type=jnp.float32,
    )
    latent_out = (final_value / final_sum[..., None]).astype(jnp.bfloat16)
    result = jnp.einsum("rnhc,hcv->rnhv", latent_out, w_uv, preferred_element_type=jnp.float32)
    return result.astype(jnp.bfloat16)[None]


def solution(mesh):
    placed = (
        P("grp", ("seq", "row"), None, None),
        P("grp", ("seq", "row"), None, None),
        P(),
        P("grp", None),
        P("grp", "row", None, "seq", None),
        P("grp", "row", None, None),
        P("seq", None, None),
        P("seq", None, None),
    )
    return jax.shard_map(
        per_device,
        mesh=mesh,
        in_specs=placed,
        out_specs=P("grp", "row", None, "seq", None),
        check_vma=False,
    )
```

profile of v0, /device:TPU:32, one launch (start us, length us, event | category | flops | bytes accessed | tf_op | source)
XLA Modules:
  0.0 160.5 jit_solution(2517873769930788412)
XLA Ops:
  6.5 0.8 fusion.39
  7.3 0.6 copy-done
  7.9 0.8 gather_fusion.1
  8.7 0.1 collective-permute-start
  8.8 3.1 %collective-permute-done = bf16[16,64,576]{2,1,0:T(8,128)(2,1)} collective-permute-done((bf16[16,64,576]{2,1,0:T(8,128)(2,1)S(1)}, bf16[16,64,576]{2,1,0:T(8,128)(2,1)}, u32[]{:S(2)}, u32[]{:S(2)}) %collective-permute-start) | collective-permute-done | bytes 1179680 | tf_op jit(solution)/shard_map/ppermute | solution.py:16
  11.9 2.1 %gather_fusion.2 = bf16[16,64,576]{2,1,0:T(8,128)(2,1)S(1)} fusion(bf16[16,64,576]{2,1,0:T(8,128)(2,1)} %collective-permute-done, s32[1024]{0:T(1024)S(1)} %pad_clamp_fusion), kind=kCustom, calls=%fused_computation.2 | custom fusion | bytes 2359360 | tf_op jit(solution)/shard_map/gather | solution.py:33
  14.0 1.2 reshape.202
  15.3 2.1 %copy.89 = bf16[16,16,4,576]{3,0,1,2:T(8,128)(2,1)S(1)} copy(bf16[16,16,4,576]{3,2,1,0:T(4,128)(2,1)} %reshape.202) | data formatting | bytes 2359296 | tf_op jit(solution)/shard_map/reshape | solution.py:36
  17.3 2.1 %copy.90 = bf16[256,4,576]{2,1,0:T(4,128)(2,1)} copy(bf16[256,4,576]{2,0,1:T(8,128)(2,1)S(1)} %bitcast.71) | data formatting | bytes 2359296 | tf_op jit(solution)/shard_map/reshape | solution.py:41
  19.4 15.1 %all-to-all-start = ((bf16[256,4,576]{2,1,0:T(4,128)(2,1)}), bf16[256,4,576]{2,1,0:T(4,128)(2,1)S(1)}, u32[]{:S(2)}, u32[]{:S(2)}) async-start(bf16[256,4,576]{2,1,0:T(4,128)(2,1)} %copy.90), calls=%async_computation | async-start | bytes 2621440 | tf_op jit(solution)/shard_map/all_to_all | solution.py:40
  34.6 1.5 fusion.8
  36.1 0.7 pad_maximum_fusion
  36.9 0.6 gather_fusion
  37.5 0.1 broadcast_compare_fusion
  37.6 34.2 %all-to-all-done = bf16[256,4,576]{2,1,0:T(4,128)(2,1)S(1)} async-done(((bf16[256,4,576]{2,1,0:T(4,128)(2,1)}), bf16[256,4,576]{2,1,0:T(4,128)(2,1)S(1)}, u32[]{:S(2)}, u32[]{:S(2)}) %all-to-all-start) | async-done | bytes 1179680 | tf_op jit(solution)/shard_map/all_to_all | solution.py:40
  71.8 2.1 %copy.91 = bf16[2,128,4,576]{3,0,2,1:T(2,128)(2,1)} copy(bf16[2,128,4,576]{3,2,0,1:T(4,128)(2,1)S(1)} %bitcast.70) | data formatting | bytes 2359296 | tf_op jit(solution)/shard_map/all_to_all | solution.py:40
  73.9 14.4 %all-gather.2.cloned.1.call-done = bf16[2,4,128,576]{3,1,0,2:T(4,128)(2,1)} async-done(((bf16[2,4,8,576]{3,1,0,2:T(4,128)(2,1)}), bf16[2,4,128,576]{3,1,0,2:T(4,128)(2,1)}) %all-gather.2.cloned.1.call-update) | async-done | bytes 1179664 | tf_op jit(solution)/shard_map/all_gather | solution.py:57
  88.3 2.8 %select_reduce_fusion = (f32[2,4,128]{2,1,0:T(4,128)S(1)}, f32[2,4,128,512]{3,2,1,0:T(8,128)S(1)}) fusion(pred[2,512]{1,0:T(4,128)(4,1)S(1)} %broadcast_compare_fusion, bf16[2,512,576,1]{2,0,1,3:T(2,128)(2,1)} %bitcast.72, bf16[2,4,128,576]{3,1,0,2:T(4,128)(2,1)} %all-gather.2.cloned.1.call-done), kind=kOutput, calls=%fused_computation.6 | convolution fusion | flops 605551616 | bytes 4461568 | tf_op jit(solution)/shard_map/rnhc,rpc->rnhp/dot_general | solution.py:59
  91.2 0.6 fusion.1
  91.8 0.8 copy.106
  92.6 4.9 %all-to-all-start.3 = ((f32[2,4,128]{1,0,2:T(2,128)}), f32[2,4,128]{1,0,2:T(2,128)S(1)}, u32[]{:S(2)}, u32[]{:S(2)}) async-start(f32[2,4,128]{1,0,2:T(2,128)} %copy.106), calls=%async_computation.3 | async-start | bytes 262144 | tf_op jit(solution)/shard_map/all_to_all | solution.py:74
  97.5 0.8 copy.96
  98.3 2.9 %slice.24 = bf16[2,512,512]{2,0,1:T(2,128)(2,1)} slice(bf16[2,512,576]{2,0,1:T(2,128)(2,1)} %bitcast.73), slice={[0:2], [0:512], [0:512]} | slice | bytes 2097152 | tf_op jit(solution)/shard_map/slice | solution.py:68
  101.2 4.1 %all-to-all-done.3 = f32[2,4,128]{1,0,2:T(2,128)S(1)} async-done(((f32[2,4,128]{1,0,2:T(2,128)}), f32[2,4,128]{1,0,2:T(2,128)S(1)}, u32[]{:S(2)}, u32[]{:S(2)}) %all-to-all-start.3) | async-done | bytes 4128 | tf_op jit(solution)/shard_map/all_to_all | solution.py:74
  105.4 0.6 copy-done.1
  106.0 3.6 %all-to-all-start.2 = ((f32[2,4,128]{1,0,2:T(2,128)}), f32[2,4,128]{1,0,2:T(2,128)S(1)}, u32[]{:S(2)}, u32[]{:S(2)}) async-start(f32[2,4,128]{1,0,2:T(2,128)} %copy.96), calls=%async_computation.2 | async-start | bytes 262144 | tf_op jit(solution)/shard_map/all_to_all | solution.py:73
  109.6 2.0 %fusion.12 = f32[2,4,128,512]{3,2,1,0:T(8,128)S(1)} fusion(f32[2,4,128,512]{3,2,1,0:T(8,128)S(1)} %get-tuple-element.12, bf16[2,512,512]{2,0,1:T(2,128)(2,1)} %slice.24, f32[2,4,128]{2,1,0:T(4,128)S(1)} %get-tuple-element.11, pred[2,512]{1,0:T(4,128)(4,1)S(1)} %broadcast_compare_fusion), kind=kOutput, calls=%fused_computation.20 | convolution fusion | flops 538968064 | bytes 5248000 | tf_op jit(solution)/shard_map/rnhp,rpc->rnhc/dot_general | solution.py:65
  111.6 2.7 %copy.95 = f32[2,4,128,512]{3,1,0,2:T(4,128)} copy(f32[2,4,128,512]{3,2,1,0:T(8,128)S(1)} %fusion.12) | data formatting | bytes 4194304 | tf_op jit(solution)/shard_map/rnhp,rpc->rnhc/dot_general | solution.py:65
  114.3 3.1 %all-to-all-done.2 = f32[2,4,128]{1,0,2:T(2,128)S(1)} async-done(((f32[2,4,128]{1,0,2:T(2,128)}), f32[2,4,128]{1,0,2:T(2,128)S(1)}, u32[]{:S(2)}, u32[]{:S(2)}) %all-to-all-start.2) | async-done | bytes 4128 | tf_op jit(solution)/shard_map/all_to_all | solution.py:73
  117.5 4.4 %all-to-all-start.1 = ((f32[2,4,128,512]{3,1,0,2:T(4,128)}), f32[2,4,128,512]{3,1,0,2:T(4,128)S(1)}, u32[]{:S(2)}, u32[]{:S(2)}) async-start(f32[2,4,128,512]{3,1,0,2:T(4,128)} %copy.95), calls=%async_computation.1 | async-start | bytes 4194304 | tf_op jit(solution)/shard_map/all_to_all | solution.py:75
  121.9 2.0 %fusion.20 = f32[2,4,8,4]{1,3,2,0:T(4,128)} fusion(bf16[2,4,8,576]{3,1,0,2:T(4,128)(2,1)} %pad_maximum_fusion, bf16[1,2,4,576]{3,2,1,0:T(4,128)(2,1)S(1)} %copy-done.4), kind=kOutput, calls=%fused_computation.30 | convolution fusion | flops 294912 | bytes 83968 | tf_op jit(solution)/shard_map/rnhc,rjc->rnhj/dot_general | solution.py:86
  123.9 0.9 copy.100
  124.8 0.5 copy-done.3
  125.3 0.7 select_reduce_fusion.1
  125.9 1.8 %copy.120 = f32[2,4,16,8]{3,2,1,0:T(8,128)} copy(f32[2,4,16,8]{1,0,3,2:T(2,128)} %bitcast.76) | data formatting | bytes 8192 | tf_op jit(solution)/shard_map/reshape | solution.py:78
  127.7 0.9 copy.119
  128.6 0.7 reduce_max.28
  129.3 0.8 copy.121
  130.1 0.7 max.13
  130.8 0.7 fusion.26
  131.4 0.9 multiply_reduce_fusion
  132.4 0.1 copy.103
  132.5 0.1 copy.110
  132.5 0.1 copy.105
  132.7 16.8 %all-to-all-done.1 = f32[2,4,128,512]{3,1,0,2:T(4,128)S(1)} async-done(((f32[2,4,128,512]{3,1,0,2:T(4,128)}), f32[2,4,128,512]{3,1,0,2:T(4,128)S(1)}, u32[]{:S(2)}, u32[]{:S(2)}) %all-to-all-start.1) | async-done | bytes 2097184 | tf_op jit(solution)/shard_map/all_to_all | solution.py:75
  149.5 1.8 %fusion = f32[2,4,8,512]{3,2,1,0:T(8,128)} fusion(f32[2,4,16,8,512]{4,1,0,3,2:T(4,128)S(1)} %bitcast.69, f32[2,4,16,8]{3,2,1,0:T(8,128)S(1)} %get-tuple-element.8), kind=kLoop, calls=%fused_computation.4 | loop fusion | flops 1015808 | bytes 2232320 | tf_op jit(solution)/shard_map/reduce_sum | solution.py:83
  151.3 1.7 %fusion.11 = bf16[1,2,4,8,128]{4,2,1,3,0:T(4,128)(2,1)S(1)} fusion(bf16[2,4,8,4]{3,1,0,2:T(4,128)(2,1)S(1)} %copy.105, bf16[8,512,128]{2,1,0:T(8,128)(2,1)} %param.15, f32[2,4,8,512]{3,2,1,0:T(8,128)} %fusion, f32[2,4,8]{1,0,2:T(2,128)S(1)} %copy.110, f32[2,4,8]{1,0,2:T(2,128)S(1)} %copy.103, bf16[2,4,576]{2,1,0:T(4,128)(2,1)S(1)} %bitcast.85), kind=kOutput, calls=%fused_computation.19 | convolution fusion | flops 8790016 | bytes 1236992 | tf_op jit(solution)/shard_map/rnhc,hcv->rnhv/dot_general | solution.py:103
  153.0 0.6 copy.111
  (26 shorter events, 0.2 us)
Async XLA Ops:
  6.5 1.3 copy-start
  6.5 2.2 %copy-start.2 = (bf16[1,2,4,8,192]{4,3,2,1,0:T(8,128)(2,1)S(1)}, bf16[1,2,4,8,192]{4,3,2,1,0:T(8,128)(2,1)}, u32[]{:S(2)}) copy-start(bf16[1,2,4,8,192]{4,3,2,1,0:T(8,128)(2,1)} %param.12) | copy-start | bytes 73732
  6.5 2.3 %copy-start.7 = (s32[1,16]{1,0:T(1,128)S(1)}, s32[1,16]{1,0:T(1,128)}, u32[]{:S(2)}) copy-start(s32[1,16]{1,0:T(1,128)} %param.11) | copy-start | bytes 196
  8.7 3.3 %collective-permute-start = (bf16[16,64,576]{2,1,0:T(8,128)(2,1)S(1)}, bf16[16,64,576]{2,1,0:T(8,128)(2,1)}, u32[]{:S(2)}, u32[]{:S(2)}) collective-permute-start(bf16[16,64,576]{2,1,0:T(8,128)(2,1)S(1)} %gather_fusion.1), channel_id=1, source_target_pairs={{0,128},{128,0},{1,129},{129,1},{2,130},{130,2},{3,131},{131,3},{4... | collective-permute-start | bytes 3538952 | tf_op jit(solution)/shard_map/ppermute | solution.py:16
  19.4 17.5 %copy-start.6 = (s32[2,16]{1,0:T(2,128)S(1)}, s32[2,16]{1,0:T(2,128)}, u32[]{:S(2)}) copy-start(s32[2,16]{1,0:T(2,128)} %param.10) | copy-start | bytes 388
  19.4 52.4 %all-to-all-start = ((bf16[256,4,576]{2,1,0:T(4,128)(2,1)}), bf16[256,4,576]{2,1,0:T(4,128)(2,1)S(1)}, u32[]{:S(2)}, u32[]{:S(2)}) async-start(bf16[256,4,576]{2,1,0:T(4,128)(2,1)} %copy.90), calls=%async_computation | async-start | bytes 2621440 | tf_op jit(solution)/shard_map/all_to_all | solution.py:40
  34.5 53.8 %all-gather.2.cloned.1.call-start = ((), (), s32[]{:S(2)}) async-start(), calls=%async_computation.4 | async-start | bytes 1392640 | tf_op jit(solution)/shard_map/all_gather | solution.py:57
  92.6 12.8 %all-to-all-start.3 = ((f32[2,4,128]{1,0,2:T(2,128)}), f32[2,4,128]{1,0,2:T(2,128)S(1)}, u32[]{:S(2)}, u32[]{:S(2)}) async-start(f32[2,4,128]{1,0,2:T(2,128)} %copy.106), calls=%async_computation.3 | async-start | bytes 262144 | tf_op jit(solution)/shard_map/all_to_all | solution.py:74
  105.4 0.6 copy-start.1
  106.0 11.4 %all-to-all-start.2 = ((f32[2,4,128]{1,0,2:T(2,128)}), f32[2,4,128]{1,0,2:T(2,128)S(1)}, u32[]{:S(2)}, u32[]{:S(2)}) async-start(f32[2,4,128]{1,0,2:T(2,128)} %copy.96), calls=%async_computation.2 | async-start | bytes 262144 | tf_op jit(solution)/shard_map/all_to_all | solution.py:73
  114.3 7.6 %copy-start.4 = (bf16[1,2,4,576]{3,2,1,0:T(4,128)(2,1)S(1)}, bf16[1,2,4,576]{3,2,1,0:T(4,128)(2,1)}, u32[]{:S(2)}) copy-start(bf16[1,2,4,576]{3,2,1,0:T(4,128)(2,1)} %param.13) | copy-start | bytes 27652
  117.5 32.1 %all-to-all-start.1 = ((f32[2,4,128,512]{3,1,0,2:T(4,128)}), f32[2,4,128,512]{3,1,0,2:T(4,128)S(1)}, u32[]{:S(2)}, u32[]{:S(2)}) async-start(f32[2,4,128,512]{3,1,0,2:T(4,128)} %copy.95), calls=%async_computation.1 | async-start | bytes 4194304 | tf_op jit(solution)/shard_map/all_to_all | solution.py:75
  124.8 0.5 copy-start.3
  129.3 22.0 %copy-start.5 = (bf16[1,2,4,576]{3,2,1,0:T(4,128)(2,1)S(1)}, bf16[1,2,4,576]{3,2,1,0:T(4,128)(2,1)}, u32[]{:S(2)}) copy-start(bf16[1,2,4,576]{3,2,1,0:T(4,128)(2,1)} %param.13) | copy-start | bytes 27652
Sparse Core Ops, SparseCore 0:
  37.9 50.4 all-gather.1
where the time goes:
time: 161 us; the launch traced here: 160 us
  waiting for transfers between devices  75.8 us (47%)
  starting transfers between devices  28.2 us (18%)
  local copies, waits for them, and re-layouts  25.2 us (16%)
  between operations  13.6 us (8%)
  matrix products  10.1 us (6%)
  other arithmetic  7.6 us (5%)
    all_to_all x1, waiting for transfers between devices, per_device(): lax.all_to_all(pieces.reshape(n_seq * n_reqs, piece_len, lat_width), ('se...  34.2 us
    all_to_all x1, waiting for transfers between devices, per_device(): lax.all_to_all(value_sum, 'seq', split_axis=2, concat_axis=2, tiled=True)  16.8 us
    all_to_all x1, starting transfers between devices, per_device(): lax.all_to_all(pieces.reshape(n_seq * n_reqs, piece_len, lat_width), ('se...  15.1 us
    all_gather x1, waiting for transfers between devices, per_device(): all_queries = lax.all_gather(own_query, 'seq', axis=2, tiled=True)  14.4 us
    all_to_all x1, starting transfers between devices, per_device(): lax.all_to_all(weight_sum, 'seq', split_axis=2, concat_axis=2, tiled=True)  4.94 us
    all_to_all x1, starting transfers between devices, per_device(): lax.all_to_all(value_sum, 'seq', split_axis=2, concat_axis=2, tiled=True)  4.39 us
    all_to_all x1, waiting for transfers between devices, per_device(): lax.all_to_all(weight_sum, 'seq', split_axis=2, concat_axis=2, tiled=True)  4.13 us
    all_to_all x1, starting transfers between devices, per_device(): lax.all_to_all(best_score, 'seq', split_axis=2, concat_axis=2, tiled=True)  3.6 us
  transfers between devices with their start and end apart: 6, of which 6 were waited for; matrix products, arithmetic and copies ran while one was open for 15% of the time, Pallas kernels for 0%

commit v1 on v0

v1 whole, which is shorter than its diff:
```python
import functools

import jax
import jax.numpy as jnp
from jax import lax
from jax.experimental import pallas as pl
from jax.experimental.pallas import tpu as pltpu
from jax.sharding import PartitionSpec as P

FILL_LOW = -1e30
LANES = 128
FOLD = 16
PARTS = 8
NT = (((1,), (1,)), ((), ()))


def smem():
    return pl.BlockSpec(memory_space=pltpu.SMEM)


def vmem():
    return pl.BlockSpec(memory_space=pltpu.VMEM)


def params(mib):
    return pltpu.CompilerParams(vmem_limit_bytes=mib << 20)


def pack_kernel(request_ref, table_ref, pool_ref, out_ref):
    n_row = out_ref.shape[0]
    rows_dev = request_ref.shape[1] // n_row
    latent = (out_ref.shape[2] - LANES) // rows_dev
    for peer in range(n_row):
        ropes = []
        for r in range(rows_dev):
            page = table_ref[0, request_ref[0, peer * rows_dev + r]]
            out_ref[peer, :, r * latent : (r + 1) * latent] = pool_ref[page, :, :latent]
            ropes.append(pool_ref[page, :, latent:])
        out_ref[peer, :, rows_dev * latent :] = jnp.concatenate(ropes, axis=1)


def query_kernel(query_ref, w_ref, out_ref):
    heads, nope, latent = w_ref.shape
    rows = query_ref.shape[0]
    plain = query_ref[:, :nope]
    head_of = lax.broadcasted_iota(jnp.int32, (rows, latent), 0) % heads
    total = jnp.zeros((rows, latent), jnp.float32)
    for h in range(heads):
        one = jnp.dot(plain, w_ref[h], preferred_element_type=jnp.float32)
        total = jnp.where(head_of == h, one, total)
    out_ref[:, :latent] = total.astype(jnp.bfloat16)
    rope = query_ref[:, nope:].astype(jnp.float32)
    second = lax.broadcasted_iota(jnp.int32, rope.shape, 0) >= rows // 2
    zero = jnp.zeros_like(rope)
    both = jnp.concatenate([jnp.where(second, zero, rope), jnp.where(second, rope, zero)], axis=1)
    out_ref[:, latent:] = both.astype(jnp.bfloat16)


def split_bf16(value, count):
    parts = []
    for _ in range(count):
        part = value.astype(jnp.bfloat16).astype(jnp.float32)
        parts.append(part)
        value = value - part
    return parts


def attend_kernel(scale, place_ref, lengths_ref, request_ref, cache_ref, *refs):
    query_refs, out_ref = refs[:-1], refs[-1]
    group, seq, row = place_ref[0], place_ref[1], place_ref[2]
    n_seq = out_ref.shape[0]
    keys = cache_ref.shape[0]
    blocks_each = n_seq // len(query_refs)
    block_rows = query_refs[0].shape[0] // blocks_each
    rows_dev = 2
    half = block_rows // rows_dev
    latent = (cache_ref.shape[1] - LANES) // rows_dev
    rows = n_seq * half
    ropes = cache_ref[:, rows_dev * latent :]
    position = lax.broadcasted_iota(jnp.int32, (1, keys), 1) + seq * keys
    lane = lax.broadcasted_iota(jnp.int32, (rows, LANES), 1)
    inner = lax.broadcasted_iota(jnp.int32, (rows, LANES), 0) % half
    folded = None
    for r in range(rows_dev):
        length = lengths_ref[group, request_ref[0, row * rows_dev + r]]
        visible = position < length
        cache = cache_ref[:, r * latent : (r + 1) * latent]
        query = jnp.concatenate(
            [
                query_ref[b * block_rows + r * half : b * block_rows + (r + 1) * half, :]
                for query_ref in query_refs
                for b in range(blocks_each)
            ],
            axis=0,
        )
        scores = lax.dot_general(query[:, :latent], cache, NT, preferred_element_type=jnp.float32)
        scores += lax.dot_general(query[:, latent:], ropes, NT, preferred_element_type=jnp.float32)
        scores = jnp.where(visible, scores * scale, FILL_LOW)
        best = jnp.max(scores, axis=1, keepdims=True)
        weights = jnp.where(visible, jnp.exp(scores - best), 0.0)
        weight_sum = jnp.sum(weights, axis=1, keepdims=True)
        value = jnp.dot(
            weights.astype(jnp.bfloat16), cache, preferred_element_type=jnp.float32
        ).astype(jnp.bfloat16)
        base = PARTS * (r * (half // FOLD) + inner // FOLD)
        stats = jnp.zeros((rows, LANES), jnp.float32)
        for j, part in enumerate(split_bf16(best, 3) + split_bf16(weight_sum, 2)):
            stats = jnp.where(lane == base + j, part, stats)
        stats = jnp.sum(stats.reshape(n_seq, half // FOLD, FOLD, LANES), axis=1)
        folded = stats if folded is None else folded + stats
        for b in range(n_seq):
            for c in range(latent // LANES):
                out_ref[seq ^ b, c * block_rows + r * half : c * block_rows + (r + 1) * half, :] = (
                    value[b * half : (b + 1) * half, c * LANES : (c + 1) * LANES]
                )
    tail = (latent // LANES) * block_rows
    for b in range(n_seq):
        out_ref[seq ^ b, tail:, :] = folded[b].astype(jnp.bfloat16)


def merge_kernel(scale, got_ref, query_ref, new_ref, w_ref, out_ref):
    n_seq = got_ref.shape[0]
    heads, latent, _ = w_ref.shape
    rows = query_ref.shape[0]
    chunks = latent // LANES
    tail = chunks * rows
    row_id = lax.broadcasted_iota(jnp.int32, (rows, LANES), 0)
    lane = lax.broadcasted_iota(jnp.int32, (rows, LANES), 1)
    base = PARTS * (row_id // FOLD)
    in_best = (lane >= base) & (lane < base + 3)
    in_sum = (lane >= base + 3) & (lane < base + 5)
    bests, sums = [], []
    for i in range(n_seq):
        stats = got_ref[i, tail:, :].astype(jnp.float32)
        stats = jnp.concatenate([stats] * (rows // FOLD), axis=0)
        bests.append(jnp.sum(jnp.where(in_best, stats, 0.0), axis=1, keepdims=True))
        sums.append(jnp.sum(jnp.where(in_sum, stats, 0.0), axis=1, keepdims=True))
    new_keys = new_ref[...].astype(jnp.float32)
    count = new_keys.shape[0]
    steps = count // 2
    new_lat = new_keys[:, :latent]
    rope = new_keys[:, latent:]
    second = lax.broadcasted_iota(jnp.int32, rope.shape, 0) >= steps
    zero = jnp.zeros_like(rope)
    new_rope = jnp.concatenate([jnp.where(second, zero, rope), jnp.where(second, rope, zero)], axis=1)
    new_scores = lax.dot_general(
        query_ref[:, :latent], new_lat.astype(jnp.bfloat16), NT, preferred_element_type=jnp.float32
    ) + lax.dot_general(
        query_ref[:, latent:], new_rope.astype(jnp.bfloat16), NT, preferred_element_type=jnp.float32
    )
    query_id = lax.broadcasted_iota(jnp.int32, (rows, count), 0)
    key_id = lax.broadcasted_iota(jnp.int32, (rows, count), 1)
    half = rows // 2
    causal = (query_id // half == key_id // steps) & (
        key_id % steps <= (query_id % half) // heads
    )
    new_scores = jnp.where(causal, new_scores * scale, FILL_LOW)
    best = jnp.max(new_scores, axis=1, keepdims=True)
    for one in bests:
        best = jnp.maximum(best, one)
    new_weights = jnp.where(causal, jnp.exp(new_scores - best), 0.0)
    total = jnp.sum(new_weights, axis=1, keepdims=True)
    new_weights = new_weights.astype(jnp.bfloat16).astype(jnp.float32)
    factors = [jnp.exp(one - best) for one in bests]
    for factor, one in zip(factors, sums):
        total = total + factor * one
    pieces = []
    for c in range(chunks):
        value = jnp.zeros((rows, LANES), jnp.float32)
        for j in range(count):
            value = value + new_weights[:, j : j + 1] * new_lat[j : j + 1, c * LANES : (c + 1) * LANES]
        for i in range(n_seq):
            value = value + factors[i] * got_ref[i, c * rows : (c + 1) * rows, :].astype(jnp.float32)
        pieces.append((value / total).astype(jnp.bfloat16))
    latent_out = jnp.concatenate(pieces, axis=1)
    head_of = lax.broadcasted_iota(jnp.int32, out_ref.shape, 0) % heads
    result = jnp.zeros(out_ref.shape, jnp.float32)
    for h in range(heads):
        one = jnp.dot(latent_out, w_ref[h], preferred_element_type=jnp.float32)
        result = jnp.where(head_of == h, one, result)
    out_ref[...] = result.astype(jnp.bfloat16)


def per_device(latent_pool, block_table, lengths, row_request, queries, new_latent, w_uk, w_uv):
    n_seq = lax.axis_size("seq")
    n_row = lax.axis_size("row")
    n_near = 4
    group = lax.axis_index("grp")
    _, rows_dev, n_new, head_dev, query_width = queries.shape
    _, page_rows, lat_width = latent_pool.shape[1:]
    latent_dim = w_uk.shape[2]
    value_dim = w_uv.shape[2]
    block_rows = rows_dev * n_new * head_dev
    scale = query_width ** (-0.5)
    swap = [(0, 1), (1, 0)]
    bf16 = jnp.bfloat16

    request = lax.ppermute(row_request, "grp", swap)
    new_keys = lax.ppermute(new_latent.reshape(rows_dev * n_new, lat_width), "grp", swap)
    packed = pl.pallas_call(
        pack_kernel,
        out_shape=jax.ShapeDtypeStruct((n_row, page_rows, rows_dev * latent_dim + LANES), bf16),
        in_specs=[smem(), smem(), vmem()],
        out_specs=vmem(),
        compiler_params=params(16),
        name="pack",
    )(request, block_table.reshape(1, -1), latent_pool[0])
    got_cache = lax.all_to_all(packed, "row", 0, 0, tiled=True)

    own_query = pl.pallas_call(
        query_kernel,
        out_shape=jax.ShapeDtypeStruct((block_rows, latent_dim + LANES), bf16),
        in_specs=[vmem(), vmem()],
        out_specs=vmem(),
        compiler_params=params(16),
        name="query",
    )(queries.reshape(block_rows, query_width), w_uk)
    near = []
    for k in range(n_near):
        route = [
            (g * n_seq + s, (1 - g) * n_seq + (s ^ k)) for g in range(2) for s in range(n_seq)
        ]
        near.append(lax.ppermute(own_query, ("grp", "seq"), route))
    near_query = jnp.concatenate(near, axis=0)
    all_query = [near_query]
    for j in range(1, n_seq // n_near):
        route = [(s, s ^ (j * n_near)) for s in range(n_seq)]
        all_query.append(lax.ppermute(near_query, "seq", route))

    place = jnp.stack([group, lax.axis_index("seq"), lax.axis_index("row")]).astype(jnp.int32)
    message = pl.pallas_call(
        functools.partial(attend_kernel, scale),
        out_shape=jax.ShapeDtypeStruct(
            (n_seq, block_rows * latent_dim // LANES + FOLD, LANES), bf16
        ),
        in_specs=[smem(), smem(), smem()] + [vmem()] * (1 + len(all_query)),
        out_specs=vmem(),
        compiler_params=params(32),
        name="attend",
    )(place, lengths, request, got_cache.reshape(n_row * page_rows, -1), *all_query)
    got = lax.all_to_all(message, "seq", 0, 0, tiled=True)

    result = pl.pallas_call(
        functools.partial(merge_kernel, scale),
        out_shape=jax.ShapeDtypeStruct((block_rows, value_dim), bf16),
        in_specs=[vmem()] * 4,
        out_specs=vmem(),
        compiler_params=params(16),
        name="merge",
    )(got, near[0], new_keys, w_uv)
    result = lax.ppermute(result, "grp", swap)
    return result.reshape(1, rows_dev, n_new, head_dev, value_dim)


def solution(mesh):
    placed = (
        P("grp", ("seq", "row"), None, None),
        P("grp", ("seq", "row"), None, None),
        P(),
        P("grp", None),
        P("grp", "row", None, "seq", None),
        P("grp", "row", None, None),
        P("seq", None, None),
        P("seq", None, None),
    )
    return jax.shard_map(
        per_device,
        mesh=mesh,
        in_specs=placed,
        out_specs=P("grp", "row", None, "seq", None),
        check_vma=False,
    )
```

time: 161 us -> 79.5 us (0.49)
  the two profiles are of different devices: /device:TPU:32 before, /device:TPU:1 now
where the time goes in v1:
time: 79.5 us; the launch traced here: 79.2 us
  waiting for transfers between devices  39.9 us (50%)
  starting transfers between devices  29.7 us (37%)
  Pallas kernels  6.78 us (9%)
  local copies, waits for them, and re-layouts  2.66 us (3%)
    ppermute x3, waiting for transfers between devices, per_device(): all_query.append(lax.ppermute(near_query, 'seq', route))  16.3 us
    all_to_all x1, waiting for transfers between devices, per_device(): got = lax.all_to_all(message, 'seq', 0, 0, tiled=True)  14.5 us
    all_to_all x1, starting transfers between devices, per_device(): got = lax.all_to_all(message, 'seq', 0, 0, tiled=True)  6.88 us
    all_to_all x1, starting transfers between devices, per_device(): got_cache = lax.all_to_all(packed, 'row', 0, 0, tiled=True)  6.58 us
    ppermute x4, waiting for transfers between devices, per_device(): near.append(lax.ppermute(own_query, ('grp', 'seq'), route))  6.15 us
    ppermute x4, starting transfers between devices, per_device(): near.append(lax.ppermute(own_query, ('grp', 'seq'), route))  4.89 us
    ppermute x3, starting transfers between devices, per_device(): all_query.append(lax.ppermute(near_query, 'seq', route))  3.95 us
    pallas_call x1, Pallas kernels, per_device(): pl.pallas_call(functools.partial(attend_kernel, scale), out_shape=jax.Sha...  3.71 us
  transfers between devices with their start and end apart: 12, of which 11 were waited for; matrix products, arithmetic and copies ran while one was open for 0% of the time, Pallas kernels for 0%

profile of v1, /device:TPU:1, one launch (start us, length us, event | category | flops | bytes accessed | tf_op | source)
XLA Modules:
  0.0 79.2 jit_solution(17841428647988771319)
XLA Ops:
  0.0 3.2 %collective-permute-start = (s32[1,16]{1,0:T(1,128)}, s32[1,16]{1,0:T(1,128)S(1)}, u32[]{:S(2)}, u32[]{:S(2)}) collective-permute-start(s32[1,16]{1,0:T(1,128)} %param.11), channel_id=1, source_target_pairs={{0,128},{128,0},{1,129},{129,1},{2,130},{130,2},{3,131},{131,3},{4... | collective-permute-start | bytes 200 | tf_op jit(solution)/shard_map/ppermute | solution.py:198
  3.2 1.0 %collective-permute-done.request_ref = s32[1,16]{1,0:T(1,128)S(1)} collective-permute-done((s32[1,16]{1,0:T(1,128)}, s32[1,16]{1,0:T(1,128)S(1)}, u32[]{:S(2)}, u32[]{:S(2)}) %collective-permute-start) | collective-permute-done | bytes 96 | tf_op jit(solution)/shard_map/ppermute | solution.py:198
  4.2 0.0 copy-start
  4.2 1.3 %copy-done = bf16[1,16,64,576]{3,2,1,0:T(8,128)(2,1)S(1)} copy-done((bf16[1,16,64,576]{3,2,1,0:T(8,128)(2,1)S(1)}, bf16[1,16,64,576]{3,2,1,0:T(8,128)(2,1)}, u32[]{:S(2)}) %copy-start) | copy-done | bytes 1179672
  5.5 0.0 copy-start.5
  5.5 0.7 copy-done.5
  6.2 1.7 %pack.1 = bf16[8,64,1152]{2,1,0:T(8,128)(2,1)} custom-call(s32[1,16]{1,0:T(1,128)S(1)} %collective-permute-done.request_ref, s32[1,16]{1,0:T(1,128)S(1)} %bitcast.11, bf16[16,64,576]{2,1,0:T(8,128)(2,1)S(1)} %bitcast.9), custom_call_target="tpu_custom_call" | custom-call | tf_op jit(solution)/shard_map/pack/pallas_call | solution.py:200
  7.9 0.0 copy-start.1
  7.9 0.0 copy-start.3
  7.9 6.6 %all-to-all-start = ((bf16[8,64,1152]{2,1,0:T(8,128)(2,1)}), bf16[8,64,1152]{2,1,0:T(8,128)(2,1)S(1)}, u32[]{:S(2)}, u32[]{:S(2)}) async-start(bf16[8,64,1152]{2,1,0:T(8,128)(2,1)} %pack.1), calls=%async_computation | async-start | bytes 2359296 | tf_op jit(solution)/shard_map/all_to_all | solution.py:208
  14.5 0.0 copy-start.4
  14.5 0.0 copy-done.1
  14.5 0.0 copy-done.3
  14.5 0.3 query.1
  14.8 0.7 collective-permute-start.1
  15.4 1.3 %collective-permute-start.2 = (bf16[64,640]{1,0:T(8,128)(2,1)S(1)}, bf16[64,640]{1,0:T(8,128)(2,1)S(1)}, u32[]{:S(2)}, u32[]{:S(2)}) collective-permute-start(bf16[64,640]{1,0:T(8,128)(2,1)S(1)} %query.1), channel_id=1, source_target_pairs={{0,136},{8,128},{16,152},{24,144},{32,168},{40,160},{48,184},{56,1... | collective-permute-start | bytes 245768 | tf_op jit(solution)/shard_map/ppermute | solution.py:223
  16.7 2.9 %collective-permute-start.3 = (bf16[64,640]{1,0:T(8,128)(2,1)S(1)}, bf16[64,640]{1,0:T(8,128)(2,1)S(1)}, u32[]{:S(2)}, u32[]{:S(2)}) collective-permute-start(bf16[64,640]{1,0:T(8,128)(2,1)S(1)} %query.1), channel_id=1, source_target_pairs={{0,144},{8,152},{16,128},{24,136},{32,176},{40,184},{48,160},{56,1... | collective-permute-start | bytes 245768 | tf_op jit(solution)/shard_map/ppermute | solution.py:223
  19.7 0.0 collective-permute-start.4
  19.7 0.0 collective-permute-done.1.query_ref
  19.7 0.2 collective-permute-done.2
  19.9 4.2 %collective-permute-done.3 = bf16[64,640]{1,0:T(8,128)(2,1)S(1)} collective-permute-done((bf16[64,640]{1,0:T(8,128)(2,1)S(1)}, bf16[64,640]{1,0:T(8,128)(2,1)S(1)}, u32[]{:S(2)}, u32[]{:S(2)}) %collective-permute-start.3) | collective-permute-done | bytes 81952 | tf_op jit(solution)/shard_map/ppermute | solution.py:223
  24.1 1.7 %collective-permute-done.4 = bf16[64,640]{1,0:T(8,128)(2,1)S(1)} collective-permute-done((bf16[64,640]{1,0:T(8,128)(2,1)S(1)}, bf16[64,640]{1,0:T(8,128)(2,1)S(1)}, u32[]{:S(2)}, u32[]{:S(2)}) %collective-permute-start.4) | collective-permute-done | bytes 81952 | tf_op jit(solution)/shard_map/ppermute | solution.py:223
  25.9 1.3 %collective-permute-start.5 = (bf16[256,640]{1,0:T(8,128)(2,1)S(1)}, bf16[256,640]{1,0:T(8,128)(2,1)S(1)}, u32[]{:S(2)}, u32[]{:S(2)}) collective-permute-start(bf16[256,640]{1,0:T(8,128)(2,1)S(1)} %constant_dynamic-update-slice_fusion.refs_0_), channel_id=1, source_target_pairs={{0,32},{8,40},{16,48},{24,56},{32,0},{40,8},{48,16},{56,24},{64,96... | collective-permute-start | bytes 983048 | tf_op jit(solution)/shard_map/ppermute | solution.py:228
  27.2 2.5 %collective-permute-start.6 = (bf16[256,640]{1,0:T(8,128)(2,1)S(1)}, bf16[256,640]{1,0:T(8,128)(2,1)S(1)}, u32[]{:S(2)}, u32[]{:S(2)}) collective-permute-start(bf16[256,640]{1,0:T(8,128)(2,1)S(1)} %constant_dynamic-update-slice_fusion.refs_0_), channel_id=1, source_target_pairs={{0,64},{8,72},{16,80},{24,88},{32,96},{40,104},{48,112},{56,120},{... | collective-permute-start | bytes 983048 | tf_op jit(solution)/shard_map/ppermute | solution.py:228
  29.6 0.2 collective-permute-start.7
  29.8 0.1 pad_add_fusion.place_ref
  29.9 5.0 %collective-permute-done.5.refs_1_ = bf16[256,640]{1,0:T(8,128)(2,1)S(1)} collective-permute-done((bf16[256,640]{1,0:T(8,128)(2,1)S(1)}, bf16[256,640]{1,0:T(8,128)(2,1)S(1)}, u32[]{:S(2)}, u32[]{:S(2)}) %collective-permute-start.5) | collective-permute-done | bytes 327712 | tf_op jit(solution)/shard_map/ppermute | solution.py:228
  34.9 9.3 %collective-permute-done.6.refs_2_ = bf16[256,640]{1,0:T(8,128)(2,1)S(1)} collective-permute-done((bf16[256,640]{1,0:T(8,128)(2,1)S(1)}, bf16[256,640]{1,0:T(8,128)(2,1)S(1)}, u32[]{:S(2)}, u32[]{:S(2)}) %collective-permute-start.6) | collective-permute-done | bytes 327712 | tf_op jit(solution)/shard_map/ppermute | solution.py:228
  44.2 2.0 %collective-permute-done.7.refs_3_ = bf16[256,640]{1,0:T(8,128)(2,1)S(1)} collective-permute-done((bf16[256,640]{1,0:T(8,128)(2,1)S(1)}, bf16[256,640]{1,0:T(8,128)(2,1)S(1)}, u32[]{:S(2)}, u32[]{:S(2)}) %collective-permute-start.7) | collective-permute-done | bytes 327712 | tf_op jit(solution)/shard_map/ppermute | solution.py:228
  46.2 0.3 all-to-all-done
  46.5 0.0 copy-done.4
  46.5 3.7 %attend.1 = bf16[16,272,128]{2,1,0:T(8,128)(2,1)} custom-call(s32[3]{0:T(128)S(1)} %pad_add_fusion.place_ref, s32[2,16]{1,0:T(2,128)S(1)} %copy-done.4, s32[1,16]{1,0:T(1,128)S(1)} %collective-permute-done.request_ref, bf16[512,1152]{1,0:T(8,128)(2,1)S(1)} %bitcast.8, bf16[256,640]{1,0:T(8,128)(2,1)S(1)} %constant_dynamic-update-slice_fusion.refs_0_, ...), custom_call_target="tpu_custom_call" | custom-call | tf_op jit(solution)/shard_map/attend/pallas_call | solution.py:231
  50.2 0.0 copy-start.6
  50.2 0.0 copy-start.2
  50.2 6.9 %all-to-all-start.1 = ((bf16[16,272,128]{2,1,0:T(8,128)(2,1)}), bf16[16,272,128]{2,1,0:T(8,128)(2,1)S(1)}, u32[]{:S(2)}, u32[]{:S(2)}) async-start(bf16[16,272,128]{2,1,0:T(8,128)(2,1)} %attend.1), calls=%async_computation.1 | async-start | bytes 2228224 | tf_op jit(solution)/shard_map/all_to_all | solution.py:241
  57.1 0.0 copy-done.6
  57.1 0.9 %collective-permute-start.8 = (bf16[8,576]{1,0:T(8,128)(2,1)S(1)}, bf16[8,576]{1,0:T(8,128)(2,1)S(1)}, u32[]{:S(2)}, u32[]{:S(2)}) collective-permute-start(bf16[8,576]{1,0:T(8,128)(2,1)S(1)} %reshape.18), channel_id=1, source_target_pairs={{0,128},{128,0},{1,129},{129,1},{2,130},{130,2},{3,131},{131,3},{4... | collective-permute-start | bytes 27656 | tf_op jit(solution)/shard_map/ppermute | solution.py:199
  58.0 0.8 %collective-permute-done.8.new_ref = bf16[8,576]{1,0:T(8,128)(2,1)S(1)} collective-permute-done((bf16[8,576]{1,0:T(8,128)(2,1)S(1)}, bf16[8,576]{1,0:T(8,128)(2,1)S(1)}, u32[]{:S(2)}, u32[]{:S(2)}) %collective-permute-start.8) | collective-permute-done | bytes 9248 | tf_op jit(solution)/shard_map/ppermute | solution.py:199
  58.8 14.5 %all-to-all-done.1.got_ref = bf16[16,272,128]{2,1,0:T(8,128)(2,1)S(1)} async-done(((bf16[16,272,128]{2,1,0:T(8,128)(2,1)}), bf16[16,272,128]{2,1,0:T(8,128)(2,1)S(1)}, u32[]{:S(2)}, u32[]{:S(2)}) %all-to-all-start.1) | async-done | bytes 1114144 | tf_op jit(solution)/shard_map/all_to_all | solution.py:241
  73.4 0.0 copy-done.2
  73.4 1.1 %merge.1 = bf16[64,128]{1,0:T(8,128)(2,1)S(1)} custom-call(bf16[16,272,128]{2,1,0:T(8,128)(2,1)S(1)} %all-to-all-done.1.got_ref, bf16[64,640]{1,0:T(8,128)(2,1)S(1)} %collective-permute-done.1.query_ref, bf16[8,576]{1,0:T(8,128)(2,1)S(1)} %collective-permute-done.8.new_ref, bf16[8,512,128]{2,1,0:T(8,128)(2,1)S(1)} %copy-done.2), custom_call_target="tpu_custom_call" | custom-call | tf_op jit(solution)/shard_map/merge/pallas_call | solution.py:243
  74.5 3.3 %collective-permute-start.9 = (bf16[64,128]{1,0:T(8,128)(2,1)S(1)}, bf16[64,128]{1,0:T(8,128)(2,1)S(1)}, u32[]{:S(2)}, u32[]{:S(2)}) collective-permute-start(bf16[64,128]{1,0:T(8,128)(2,1)S(1)} %merge.1), channel_id=1, source_target_pairs={{0,128},{128,0},{1,129},{129,1},{2,130},{130,2},{3,131},{131,3},{4... | collective-permute-start | bytes 49160 | tf_op jit(solution)/shard_map/ppermute | solution.py:251
  77.8 0.8 %collective-permute-done.9 = bf16[64,128]{1,0:T(8,128)(2,1)S(1)} collective-permute-done((bf16[64,128]{1,0:T(8,128)(2,1)S(1)}, bf16[64,128]{1,0:T(8,128)(2,1)S(1)}, u32[]{:S(2)}, u32[]{:S(2)}) %collective-permute-start.9) | collective-permute-done | bytes 16416 | tf_op jit(solution)/shard_map/ppermute | solution.py:251
  78.6 0.6 copy.13
  (5 shorter events, 0.1 us)
Async XLA Ops:
  0.0 4.2 %collective-permute-start = (s32[1,16]{1,0:T(1,128)}, s32[1,16]{1,0:T(1,128)S(1)}, u32[]{:S(2)}, u32[]{:S(2)}) collective-permute-start(s32[1,16]{1,0:T(1,128)} %param.11), channel_id=1, source_target_pairs={{0,128},{128,0},{1,129},{129,1},{2,130},{130,2},{3,131},{131,3},{4... | collective-permute-start | bytes 200 | tf_op jit(solution)/shard_map/ppermute | solution.py:198
  4.2 1.3 %copy-start = (bf16[1,16,64,576]{3,2,1,0:T(8,128)(2,1)S(1)}, bf16[1,16,64,576]{3,2,1,0:T(8,128)(2,1)}, u32[]{:S(2)}) copy-start(bf16[1,16,64,576]{3,2,1,0:T(8,128)(2,1)} %param.8) | copy-start | bytes 3538948
  5.5 0.7 copy-start.5
  7.9 6.6 %copy-start.1 = (bf16[8,128,512]{2,1,0:T(8,128)(2,1)S(1)}, bf16[8,128,512]{2,1,0:T(8,128)(2,1)}, u32[]{:S(2)}) copy-start(bf16[8,128,512]{2,1,0:T(8,128)(2,1)} %w_ref.2) | copy-start | bytes 3145732
  7.9 6.6 %copy-start.3 = (bf16[1,2,4,8,192]{4,3,2,1,0:T(8,128)(2,1)S(1)}, bf16[1,2,4,8,192]{4,3,2,1,0:T(8,128)(2,1)}, u32[]{:S(2)}) copy-start(bf16[1,2,4,8,192]{4,3,2,1,0:T(8,128)(2,1)} %param.12) | copy-start | bytes 73732
  7.9 38.6 %all-to-all-start = ((bf16[8,64,1152]{2,1,0:T(8,128)(2,1)}), bf16[8,64,1152]{2,1,0:T(8,128)(2,1)S(1)}, u32[]{:S(2)}, u32[]{:S(2)}) async-start(bf16[8,64,1152]{2,1,0:T(8,128)(2,1)} %pack.1), calls=%async_computation | async-start | bytes 2359296 | tf_op jit(solution)/shard_map/all_to_all | solution.py:208
  14.5 32.0 %copy-start.4 = (s32[2,16]{1,0:T(2,128)S(1)}, s32[2,16]{1,0:T(2,128)}, u32[]{:S(2)}) copy-start(s32[2,16]{1,0:T(2,128)} %lengths_ref.1) | copy-start | bytes 388
  14.8 4.9 %collective-permute-start.1 = (bf16[64,640]{1,0:T(8,128)(2,1)S(1)}, bf16[64,640]{1,0:T(8,128)(2,1)S(1)}, u32[]{:S(2)}, u32[]{:S(2)}) collective-permute-start(bf16[64,640]{1,0:T(8,128)(2,1)S(1)} %query.1), channel_id=1, source_target_pairs={{0,128},{8,136},{16,144},{24,152},{32,160},{40,168},{48,176},{56,1... | collective-permute-start | bytes 245768 | tf_op jit(solution)/shard_map/ppermute | solution.py:223
  15.4 4.4 %collective-permute-start.2 = (bf16[64,640]{1,0:T(8,128)(2,1)S(1)}, bf16[64,640]{1,0:T(8,128)(2,1)S(1)}, u32[]{:S(2)}, u32[]{:S(2)}) collective-permute-start(bf16[64,640]{1,0:T(8,128)(2,1)S(1)} %query.1), channel_id=1, source_target_pairs={{0,136},{8,128},{16,152},{24,144},{32,168},{40,160},{48,184},{56,1... | collective-permute-start | bytes 245768 | tf_op jit(solution)/shard_map/ppermute | solution.py:223
  16.7 7.4 %collective-permute-start.3 = (bf16[64,640]{1,0:T(8,128)(2,1)S(1)}, bf16[64,640]{1,0:T(8,128)(2,1)S(1)}, u32[]{:S(2)}, u32[]{:S(2)}) collective-permute-start(bf16[64,640]{1,0:T(8,128)(2,1)S(1)} %query.1), channel_id=1, source_target_pairs={{0,144},{8,152},{16,128},{24,136},{32,176},{40,184},{48,160},{56,1... | collective-permute-start | bytes 245768 | tf_op jit(solution)/shard_map/ppermute | solution.py:223
  19.7 6.2 %collective-permute-start.4 = (bf16[64,640]{1,0:T(8,128)(2,1)S(1)}, bf16[64,640]{1,0:T(8,128)(2,1)S(1)}, u32[]{:S(2)}, u32[]{:S(2)}) collective-permute-start(bf16[64,640]{1,0:T(8,128)(2,1)S(1)} %query.1), channel_id=1, source_target_pairs={{0,152},{8,144},{16,136},{24,128},{32,184},{40,176},{48,168},{56,1... | collective-permute-start | bytes 245768 | tf_op jit(solution)/shard_map/ppermute | solution.py:223
  25.9 9.1 %collective-permute-start.5 = (bf16[256,640]{1,0:T(8,128)(2,1)S(1)}, bf16[256,640]{1,0:T(8,128)(2,1)S(1)}, u32[]{:S(2)}, u32[]{:S(2)}) collective-permute-start(bf16[256,640]{1,0:T(8,128)(2,1)S(1)} %constant_dynamic-update-slice_fusion.refs_0_), channel_id=1, source_target_pairs={{0,32},{8,40},{16,48},{24,56},{32,0},{40,8},{48,16},{56,24},{64,96... | collective-permute-start | bytes 983048 | tf_op jit(solution)/shard_map/ppermute | solution.py:228
  27.2 17.0 %collective-permute-start.6 = (bf16[256,640]{1,0:T(8,128)(2,1)S(1)}, bf16[256,640]{1,0:T(8,128)(2,1)S(1)}, u32[]{:S(2)}, u32[]{:S(2)}) collective-permute-start(bf16[256,640]{1,0:T(8,128)(2,1)S(1)} %constant_dynamic-update-slice_fusion.refs_0_), channel_id=1, source_target_pairs={{0,64},{8,72},{16,80},{24,88},{32,96},{40,104},{48,112},{56,120},{... | collective-permute-start | bytes 983048 | tf_op jit(solution)/shard_map/ppermute | solution.py:228
  29.6 16.6 %collective-permute-start.7 = (bf16[256,640]{1,0:T(8,128)(2,1)S(1)}, bf16[256,640]{1,0:T(8,128)(2,1)S(1)}, u32[]{:S(2)}, u32[]{:S(2)}) collective-permute-start(bf16[256,640]{1,0:T(8,128)(2,1)S(1)} %constant_dynamic-update-slice_fusion.refs_0_), channel_id=1, source_target_pairs={{0,96},{8,104},{16,112},{24,120},{32,64},{40,72},{48,80},{56,88},{... | collective-permute-start | bytes 983048 | tf_op jit(solution)/shard_map/ppermute | solution.py:228
  50.2 6.9 %copy-start.6 = (bf16[1,2,4,576]{3,2,1,0:T(4,128)(2,1)S(1)}, bf16[1,2,4,576]{3,2,1,0:T(4,128)(2,1)}, u32[]{:S(2)}) copy-start(bf16[1,2,4,576]{3,2,1,0:T(4,128)(2,1)} %param.13) | copy-start | bytes 27652
  50.2 23.2 %copy-start.2 = (bf16[8,512,128]{2,1,0:T(8,128)(2,1)S(1)}, bf16[8,512,128]{2,1,0:T(8,128)(2,1)}, u32[]{:S(2)}) copy-start(bf16[8,512,128]{2,1,0:T(8,128)(2,1)} %w_ref.3) | copy-start | bytes 3145732
  50.2 23.2 %all-to-all-start.1 = ((bf16[16,272,128]{2,1,0:T(8,128)(2,1)}), bf16[16,272,128]{2,1,0:T(8,128)(2,1)S(1)}, u32[]{:S(2)}, u32[]{:S(2)}) async-start(bf16[16,272,128]{2,1,0:T(8,128)(2,1)} %attend.1), calls=%async_computation.1 | async-start | bytes 2228224 | tf_op jit(solution)/shard_map/all_to_all | solution.py:241
  57.1 1.7 %collective-permute-start.8 = (bf16[8,576]{1,0:T(8,128)(2,1)S(1)}, bf16[8,576]{1,0:T(8,128)(2,1)S(1)}, u32[]{:S(2)}, u32[]{:S(2)}) collective-permute-start(bf16[8,576]{1,0:T(8,128)(2,1)S(1)} %reshape.18), channel_id=1, source_target_pairs={{0,128},{128,0},{1,129},{129,1},{2,130},{130,2},{3,131},{131,3},{4... | collective-permute-start | bytes 27656 | tf_op jit(solution)/shard_map/ppermute | solution.py:199
  74.5 4.2 %collective-permute-start.9 = (bf16[64,128]{1,0:T(8,128)(2,1)S(1)}, bf16[64,128]{1,0:T(8,128)(2,1)S(1)}, u32[]{:S(2)}, u32[]{:S(2)}) collective-permute-start(bf16[64,128]{1,0:T(8,128)(2,1)S(1)} %merge.1), channel_id=1, source_target_pairs={{0,128},{128,0},{1,129},{129,1},{2,130},{130,2},{3,131},{131,3},{4... | collective-permute-start | bytes 49160 | tf_op jit(solution)/shard_map/ppermute | solution.py:251

commit v2 on v1

v2 whole, which is shorter than its diff:
```python
import functools

import jax
import jax.numpy as jnp
from jax import lax
from jax.experimental import pallas as pl
from jax.experimental.pallas import tpu as pltpu
from jax.sharding import PartitionSpec as P

FILL_LOW = -1e30
LOG2_E = 1.4426950408889634
LANES = 128
FOLD = 16
PARTS = 8
N_NEAR = 4
NT = (((1,), (1,)), ((), ()))


def smem():
    return pl.BlockSpec(memory_space=pltpu.SMEM)


def vmem():
    return pl.BlockSpec(memory_space=pltpu.VMEM)


def params(mib):
    return pltpu.CompilerParams(vmem_limit_bytes=mib << 20)


def pack_kernel(request_ref, table_ref, pool_ref, out_ref, packed, sems):
    n_peer, half_page, _ = packed.shape
    latent = packed.shape[2] // 2 - LANES // 2
    n_row = n_peer // 2
    stores = []
    for peer in range(n_peer):
        page = table_ref[0, request_ref[0, peer % n_row * 2 + peer // n_row]]
        packed[peer, :, :latent] = pool_ref[page, :half_page, :latent]
        packed[peer, :, latent : latent + LANES] = jnp.concatenate(
            [pool_ref[page, :half_page, latent:], pool_ref[page, half_page:, latent:]], axis=1
        )
        packed[peer, :, latent + LANES :] = pool_ref[page, half_page:, :latent]
        stores.append(pltpu.make_async_copy(packed.at[peer], out_ref.at[peer], sems.at[peer]))
        stores[peer].start()
    for store in stores:
        store.wait()


def query_kernel(place_ref, lengths_ref, request_ref, query_ref, w_ref, out_ref, bias_ref):
    group, seq, row = place_ref[0], place_ref[1], place_ref[2]
    heads, nope, latent = w_ref.shape
    rows = query_ref.shape[0]
    n_row = request_ref.shape[1] // 2
    keys = bias_ref.shape[1]
    half_page = keys // (2 * n_row)
    pair = seq // N_NEAR % 2
    length = lengths_ref[group, request_ref[0, row * 2 + pair]]
    key_id = lax.broadcasted_iota(jnp.int32, (1, keys), 1)
    source = key_id // half_page
    block = (seq + (source // n_row - pair) * N_NEAR) * n_row + source % n_row
    for h in range(2):
        position = block * (2 * half_page) + h * half_page + key_id % half_page
        bias_ref[h : h + 1, :] = jnp.where(position < length, 0.0, FILL_LOW)
    plain = query_ref[:, :nope]
    head_of = lax.broadcasted_iota(jnp.int32, (rows, latent), 0) % heads
    total = jnp.zeros((rows, latent), jnp.float32)
    for h in range(heads):
        one = jnp.dot(plain, w_ref[h], preferred_element_type=jnp.float32)
        total = jnp.where(head_of == h, one, total)
    total = total.astype(jnp.bfloat16)
    rope = query_ref[:, nope:]
    rope = jnp.concatenate([rope, rope], axis=1)
    for r in range(2):
        part = slice(r * rows // 2, (r + 1) * rows // 2)
        out_ref[r, :, :latent] = total[part]
        out_ref[r, :, latent:] = rope[part]


def split_bf16(value, count):
    parts = []
    for _ in range(count):
        part = value.astype(jnp.bfloat16).astype(jnp.float32)
        parts.append(part)
        value = value - part
    return parts


def attend_kernel(scale2, bias_ref, cache_ref, *refs):
    query_refs, (out_ref, score_ref, weight_ref, send_ref, sems) = refs[:-5], refs[-5:]
    seq = lax.axis_index("seq")
    n_seq = out_ref.shape[0]
    n_far = len(query_refs)
    rows = query_refs[0].shape[0] // N_NEAR
    latent = (cache_ref.shape[1] - LANES) // 2
    chunks = latent // LANES
    lane = lax.broadcasted_iota(jnp.int32, (rows, LANES), 1)
    base = PARTS * (lax.broadcasted_iota(jnp.int32, (rows, LANES), 0) // FOLD)
    far, near = seq // N_NEAR, seq % N_NEAR
    owner = [
        (far + n_far - b // N_NEAR) % n_far * N_NEAR + (near ^ (b % N_NEAR)) for b in range(n_seq)
    ]
    query = jnp.concatenate([ref[...] for ref in query_refs], axis=0)
    plain, rope = query[:, :latent], query[:, latent:]
    low = lax.broadcasted_iota(jnp.int32, rope.shape, 1) < LANES // 2
    zero = jnp.zeros_like(rope)
    for h in range(2):
        if h == 0:
            side = jnp.concatenate([plain, jnp.where(low, rope, zero)], axis=1)
        else:
            side = jnp.concatenate([jnp.where(low, zero, rope), plain], axis=1)
        score_ref[h] = lax.dot_general(
            side, cache_ref[:, h * latent : (h + 1) * latent + LANES], NT,
            preferred_element_type=jnp.float32,
        )
    for b in range(n_seq):
        block = slice(b * rows, (b + 1) * rows)
        scores = [score_ref[h, block] + bias_ref[h : h + 1, :] for h in range(2)]
        best = jnp.max(jnp.maximum(*scores), axis=1, keepdims=True)
        weights = [jnp.exp2((one - best) * scale2) for one in scores]
        for h in range(2):
            weight_ref[h, block] = weights[h].astype(jnp.bfloat16)
        weight_sum = jnp.sum(weights[0] + weights[1], axis=1, keepdims=True)
        stats = jnp.zeros((rows, LANES), jnp.float32)
        for j, part in enumerate(split_bf16(best * scale2, 3) + split_bf16(weight_sum, 2)):
            stats = jnp.where(lane == base + j, part, stats)
        stats = sum(stats[i * FOLD : (i + 1) * FOLD] for i in range(rows // FOLD))
        send_ref[b, chunks * rows :, :] = stats.astype(jnp.bfloat16)
    value = jnp.dot(weight_ref[0], cache_ref[:, :latent], preferred_element_type=jnp.float32)
    value += jnp.dot(
        weight_ref[1], cache_ref[:, latent + LANES :], preferred_element_type=jnp.float32
    )
    value = value.astype(jnp.bfloat16)
    sends = []
    for b in range(n_seq):
        for c in range(chunks):
            send_ref[b, c * rows : (c + 1) * rows, :] = (
                value[b * rows : (b + 1) * rows, c * LANES : (c + 1) * LANES]
            )
        sends.append(pltpu.make_async_copy(send_ref.at[b], out_ref.at[owner[b]], sems.at[b]))
        sends[b].start()
    for send in sends:
        send.wait()


def merge_kernel(scale2, got_ref, query_ref, new_ref, w_ref, out_ref):
    n_seq = got_ref.shape[0]
    heads, latent, _ = w_ref.shape
    rows = query_ref.shape[1]
    chunks = latent // LANES
    tail = chunks * rows
    lane = lax.broadcasted_iota(jnp.int32, (rows, LANES), 1)
    base = PARTS * (lax.broadcasted_iota(jnp.int32, (rows, LANES), 0) // FOLD)
    in_best = (lane >= base) & (lane < base + 3)
    in_sum = (lane >= base + 3) & (lane < base + 5)
    count = new_ref.shape[0] // 2
    token = lax.broadcasted_iota(jnp.int32, (rows, count), 0) // heads
    causal = lax.broadcasted_iota(jnp.int32, (rows, count), 1) <= token
    latent_out = []
    for r in range(2):
        sources = [i for i in range(n_seq) if i // N_NEAR % 2 == r]
        bests, sums = [], []
        for i in sources:
            stats = got_ref[i, tail:, :].astype(jnp.float32)
            stats = jnp.concatenate([stats] * (rows // FOLD), axis=0)
            bests.append(jnp.sum(jnp.where(in_best, stats, 0.0), axis=1, keepdims=True))
            sums.append(jnp.sum(jnp.where(in_sum, stats, 0.0), axis=1, keepdims=True))
        new_keys = new_ref[...].astype(jnp.float32)[r * count : (r + 1) * count]
        new_lat, rope = new_keys[:, :latent], new_keys[:, latent:]
        keys = jnp.concatenate([new_keys, jnp.zeros_like(rope)], axis=1).astype(jnp.bfloat16)
        new_scores = lax.dot_general(query_ref[r], keys, NT, preferred_element_type=jnp.float32)
        new_scores = jnp.where(causal, new_scores * scale2, FILL_LOW)
        best = jnp.max(new_scores, axis=1, keepdims=True)
        for one in bests:
            best = jnp.maximum(best, one)
        new_weights = jnp.where(causal, jnp.exp2(new_scores - best), 0.0)
        total = jnp.sum(new_weights, axis=1, keepdims=True)
        new_weights = new_weights.astype(jnp.bfloat16).astype(jnp.float32)
        factors = [jnp.exp2(one - best) for one in bests]
        for factor, one in zip(factors, sums):
            total = total + factor * one
        pieces = []
        for c in range(chunks):
            value = jnp.zeros((rows, LANES), jnp.float32)
            for j in range(count):
                value = value + (
                    new_weights[:, j : j + 1] * new_lat[j : j + 1, c * LANES : (c + 1) * LANES]
                )
            for factor, i in zip(factors, sources):
                value = value + factor * got_ref[i, c * rows : (c + 1) * rows].astype(jnp.float32)
            pieces.append((value / total).astype(jnp.bfloat16))
        latent_out.append(jnp.concatenate(pieces, axis=1))
    latent_out = jnp.concatenate(latent_out, axis=0)
    head_of = lax.broadcasted_iota(jnp.int32, out_ref.shape, 0) % heads
    result = jnp.zeros(out_ref.shape, jnp.float32)
    for h in range(heads):
        one = jnp.dot(latent_out, w_ref[h], preferred_element_type=jnp.float32)
        result = jnp.where(head_of == h, one, result)
    out_ref[...] = result.astype(jnp.bfloat16)


def per_device(latent_pool, block_table, lengths, row_request, queries, new_latent, w_uk, w_uv):
    n_seq = lax.axis_size("seq")
    n_row = lax.axis_size("row")
    group = lax.axis_index("grp")
    _, rows_dev, n_new, head_dev, query_width = queries.shape
    _, page_rows, lat_width = latent_pool.shape[1:]
    latent_dim = w_uk.shape[2]
    value_dim = w_uv.shape[2]
    half_rows = n_new * head_dev
    block_rows = rows_dev * half_rows
    keys = n_row * page_rows
    scale2 = query_width ** (-0.5) * LOG2_E
    swap = [(0, 1), (1, 0)]
    bf16 = jnp.bfloat16

    pool = lax.ppermute(latent_pool[0], "grp", swap)
    table = lax.ppermute(block_table.reshape(1, -1), "grp", swap)
    packed_shape = (2 * n_row, page_rows // 2, 2 * latent_dim + LANES)
    packed = pl.pallas_call(
        pack_kernel,
        out_shape=jax.ShapeDtypeStruct(packed_shape, bf16),
        in_specs=[smem(), smem(), vmem()],
        out_specs=pl.BlockSpec(memory_space=pl.ANY),
        scratch_shapes=[pltpu.VMEM(packed_shape, bf16), pltpu.SemaphoreType.DMA((2 * n_row,))],
        compiler_params=params(16),
        name="pack",
    )(row_request, table, pool)
    pairs = [
        [(base + pair * N_NEAR) * n_row + row for pair in range(2) for row in range(n_row)]
        for base in range(n_seq)
        if base // N_NEAR % 2 == 0
    ]
    got_cache = lax.all_to_all(
        packed, ("seq", "row"), 0, 0, axis_index_groups=pairs, tiled=True
    )

    place = jnp.stack([1 - group, lax.axis_index("seq"), lax.axis_index("row")]).astype(jnp.int32)
    own_query, bias = pl.pallas_call(
        query_kernel,
        out_shape=(
            jax.ShapeDtypeStruct((rows_dev, half_rows, latent_dim + LANES), bf16),
            jax.ShapeDtypeStruct((2, keys), jnp.float32),
        ),
        in_specs=[smem()] * 3 + [vmem()] * 2,
        out_specs=(vmem(), vmem()),
        compiler_params=params(16),
        name="query",
    )(place, lengths, row_request, queries.reshape(block_rows, query_width), w_uk)
    near = [own_query]
    for k in range(1, N_NEAR):
        near.append(lax.ppermute(own_query, "seq", [(s, s ^ k) for s in range(n_seq)]))
    near_query = jnp.concatenate(near, axis=1)
    pair = lax.axis_index("seq") // N_NEAR % 2
    same, other = (
        lax.dynamic_index_in_dim(near_query, one, 0, keepdims=False) for one in (pair, 1 - pair)
    )
    all_query = [same]
    for j in range(1, n_seq // N_NEAR):
        route = [(s, (s + j * N_NEAR) % n_seq) for s in range(n_seq)]
        all_query.append(lax.ppermute(other if j % 2 else same, "seq", route))

    send_shape = (n_seq, half_rows * latent_dim // LANES + FOLD, LANES)
    message = pl.pallas_call(
        functools.partial(attend_kernel, scale2),
        out_shape=jax.ShapeDtypeStruct(send_shape, bf16),
        in_specs=[vmem()] * (2 + len(all_query)),
        out_specs=pl.BlockSpec(memory_space=pl.ANY),
        scratch_shapes=[
            pltpu.VMEM((2, n_seq * half_rows, keys), jnp.float32),
            pltpu.VMEM((2, n_seq * half_rows, keys), bf16),
            pltpu.VMEM(send_shape, bf16),
            pltpu.SemaphoreType.DMA((n_seq,)),
        ],
        compiler_params=params(32),
        name="attend",
    )(bias, got_cache.reshape(keys, -1), *all_query)
    got = lax.all_to_all(message, "seq", 0, 0, tiled=True)

    result = pl.pallas_call(
        functools.partial(merge_kernel, scale2),
        out_shape=jax.ShapeDtypeStruct((block_rows, value_dim), bf16),
        in_specs=[vmem()] * 4,
        out_specs=vmem(),
        compiler_params=params(16),
        name="merge",
    )(got, own_query, new_latent.reshape(rows_dev * n_new, lat_width), w_uv)
    return result.reshape(1, rows_dev, n_new, head_dev, value_dim)


def solution(mesh):
    placed = (
        P("grp", ("seq", "row"), None, None),
        P("grp", ("seq", "row"), None, None),
        P(),
        P("grp", None),
        P("grp", "row", None, "seq", None),
        P("grp", "row", None, None),
        P("seq", None, None),
        P("seq", None, None),
    )
    return jax.shard_map(
        per_device,
        mesh=mesh,
        in_specs=placed,
        out_specs=P("grp", "row", None, "seq", None),
        check_vma=False,
    )
```

time: 79.5 us -> 66.5 us (0.84)
  the two profiles are of different devices: /device:TPU:1 before, /device:TPU:32 now
where the time goes in v2:
time: 66.5 us; the launch traced here: 66.2 us
  waiting for transfers between devices  31.2 us (47%)
  starting transfers between devices  27.1 us (41%)
  Pallas kernels  6.89 us (10%)
  local copies, waits for them, and re-layouts  0.8 us (1%)
    ppermute x3, waiting for transfers between devices, per_device(): all_query.append(lax.ppermute(other if j % 2 else same, 'seq', route))  12.4 us
    all_to_all x1, waiting for transfers between devices, per_device(): got = lax.all_to_all(message, 'seq', 0, 0, tiled=True)  10.4 us
    all_to_all x1, starting transfers between devices, per_device(): lax.all_to_all(packed, ('seq', 'row'), 0, 0, axis_index_groups=pairs, til...  9.66 us
    all_to_all x1, starting transfers between devices, per_device(): got = lax.all_to_all(message, 'seq', 0, 0, tiled=True)  6.75 us
    ppermute x3, starting transfers between devices, per_device(): all_query.append(lax.ppermute(other if j % 2 else same, 'seq', route))  5.44 us
    ppermute x3, waiting for transfers between devices, per_device(): lax.ppermute(own_query, 'seq', [(s, s ^ k) for s in range(n_seq)])  5.38 us
    ppermute x3, starting transfers between devices, per_device(): lax.ppermute(own_query, 'seq', [(s, s ^ k) for s in range(n_seq)])  4.79 us
    pallas_call x1, Pallas kernels, per_device(): pl.pallas_call(functools.partial(attend_kernel, scale2), out_shape=jax.Sh...  2.79 us
  transfers between devices with their start and end apart: 10, of which 7 were waited for; matrix products, arithmetic and copies ran while one was open for 0% of the time, Pallas kernels for 1%

profile of v2, /device:TPU:32, one launch (start us, length us, event | category | flops | bytes accessed | tf_op | source)
XLA Modules:
  0.0 66.2 jit_solution(2279494077577570146)
XLA Ops:
  0.0 0.0 collective-permute-start.1
  0.0 0.5 collective-permute-start
  0.5 2.7 %collective-permute-done.table_ref = s32[1,16]{1,0:T(1,128)S(1)} collective-permute-done((s32[1,16]{1,0:T(1,128)}, s32[1,16]{1,0:T(1,128)S(1)}, u32[]{:S(2)}, u32[]{:S(2)}) %collective-permute-start) | collective-permute-done | bytes 96 | tf_op jit(solution)/shard_map/ppermute | solution.py:217
  3.2 0.0 collective-permute-done.1.pool_ref
  3.2 0.0 copy-start.3
  3.3 0.7 copy-done.3
  3.9 1.8 %pack.1 = bf16[16,32,1152]{2,1,0:T(8,128)(2,1)} custom-call(s32[1,16]{1,0:T(1,128)S(1)} %copy-done.3, s32[1,16]{1,0:T(1,128)S(1)} %collective-permute-done.table_ref, bf16[16,64,576]{2,1,0:T(8,128)(2,1)S(1)} %collective-permute-done.1.pool_ref), custom_call_target="tpu_custom_call" | custom-call | tf_op jit(solution)/shard_map/pack/pallas_call | solution.py:219
  5.7 0.0 copy-start
  5.7 0.0 copy-start.2
  5.7 0.0 copy-start.4
  5.8 0.0 copy-start.5
  5.8 9.7 %all-to-all-start = ((bf16[16,32,1152]{2,1,0:T(8,128)(2,1)}), bf16[16,32,1152]{2,1,0:T(8,128)(2,1)S(1)}, u32[]{:S(2)}, u32[]{:S(2)}) async-start(bf16[16,32,1152]{2,1,0:T(8,128)(2,1)} %pack.1), calls=%async_computation | async-start | bytes 2359296 | tf_op jit(solution)/shard_map/all_to_all | solution.py:233
  15.4 0.1 pad_add_fusion.place_ref
  15.5 0.0 copy-done
  15.5 0.0 copy-done.2
  15.5 0.0 copy-done.4
  15.5 0.0 copy-done.5
  15.5 0.9 %query.1 = (bf16[2,32,640]{2,1,0:T(8,128)(2,1)S(1)}, f32[2,512]{1,0:T(2,128)S(1)}) custom-call(s32[3]{0:T(128)S(1)} %pad_add_fusion.place_ref, s32[2,16]{1,0:T(2,128)S(1)} %copy-done.5, s32[1,16]{1,0:T(1,128)S(1)} %copy-done.4, bf16[64,192]{1,0:T(8,128)(2,1)S(1)} %bitcast.13, bf16[8,128,512]{2,1,0:T(8,128)(2,1)S(1)} %copy-done), custom_call_target="tpu_custom_call" | custom-call | tf_op jit(solution)/shard_map/query/pallas_call | solution.py:238
  16.4 1.7 %collective-permute-start.2 = (bf16[2,32,640]{2,1,0:T(8,128)(2,1)S(1)}, bf16[2,32,640]{2,1,0:T(8,128)(2,1)S(1)}, u32[]{:S(2)}, u32[]{:S(2)}) collective-permute-start(bf16[2,32,640]{2,1,0:T(8,128)(2,1)S(1)} %get-tuple-element.8.query_ref), channel_id=1, source_target_pairs={{0,8},{8,0},{16,24},{24,16},{32,40},{40,32},{48,56},{56,48},{64,72... | collective-permute-start | bytes 245768 | tf_op jit(solution)/shard_map/ppermute | solution.py:251
  18.1 2.9 %collective-permute-start.3 = (bf16[2,32,640]{2,1,0:T(8,128)(2,1)S(1)}, bf16[2,32,640]{2,1,0:T(8,128)(2,1)S(1)}, u32[]{:S(2)}, u32[]{:S(2)}) collective-permute-start(bf16[2,32,640]{2,1,0:T(8,128)(2,1)S(1)} %get-tuple-element.8.query_ref), channel_id=1, source_target_pairs={{0,16},{8,24},{16,0},{24,8},{32,48},{40,56},{48,32},{56,40},{64,80... | collective-permute-start | bytes 245768 | tf_op jit(solution)/shard_map/ppermute | solution.py:251
  21.0 0.2 collective-permute-start.4
  21.2 0.0 collective-permute-done.2
  21.2 3.5 %collective-permute-done.3 = bf16[2,32,640]{2,1,0:T(8,128)(2,1)S(1)} collective-permute-done((bf16[2,32,640]{2,1,0:T(8,128)(2,1)S(1)}, bf16[2,32,640]{2,1,0:T(8,128)(2,1)S(1)}, u32[]{:S(2)}, u32[]{:S(2)}) %collective-permute-start.3) | collective-permute-done | bytes 81952 | tf_op jit(solution)/shard_map/ppermute | solution.py:251
  24.7 1.9 %collective-permute-done.4 = bf16[2,32,640]{2,1,0:T(8,128)(2,1)S(1)} collective-permute-done((bf16[2,32,640]{2,1,0:T(8,128)(2,1)S(1)}, bf16[2,32,640]{2,1,0:T(8,128)(2,1)S(1)}, u32[]{:S(2)}, u32[]{:S(2)}) %collective-permute-start.4) | collective-permute-done | bytes 81952 | tf_op jit(solution)/shard_map/ppermute | solution.py:251
  26.7 1.5 %collective-permute-start.5 = (bf16[128,640]{1,0:T(8,128)(2,1)S(1)}, bf16[128,640]{1,0:T(8,128)(2,1)S(1)}, u32[]{:S(2)}, u32[]{:S(2)}) collective-permute-start(bf16[128,640]{1,0:T(8,128)(2,1)S(1)} %get-tuple-element.9), channel_id=1, source_target_pairs={{0,32},{8,40},{16,48},{24,56},{32,64},{40,72},{48,80},{56,88},{64,... | collective-permute-start | bytes 491528 | tf_op jit(solution)/shard_map/ppermute | solution.py:260
  28.2 2.7 %collective-permute-start.6 = (bf16[128,640]{1,0:T(8,128)(2,1)S(1)}, bf16[128,640]{1,0:T(8,128)(2,1)S(1)}, u32[]{:S(2)}, u32[]{:S(2)}) collective-permute-start(bf16[128,640]{1,0:T(8,128)(2,1)S(1)} %get-tuple-element.10.refs_0_), channel_id=1, source_target_pairs={{0,64},{8,72},{16,80},{24,88},{32,96},{40,104},{48,112},{56,120},{... | collective-permute-start | bytes 491528 | tf_op jit(solution)/shard_map/ppermute | solution.py:260
  30.9 1.2 %collective-permute-start.7 = (bf16[128,640]{1,0:T(8,128)(2,1)S(1)}, bf16[128,640]{1,0:T(8,128)(2,1)S(1)}, u32[]{:S(2)}, u32[]{:S(2)}) collective-permute-start(bf16[128,640]{1,0:T(8,128)(2,1)S(1)} %get-tuple-element.9), channel_id=1, source_target_pairs={{0,96},{8,104},{16,112},{24,120},{32,0},{40,8},{48,16},{56,24},{64... | collective-permute-start | bytes 491528 | tf_op jit(solution)/shard_map/ppermute | solution.py:260
  32.1 6.3 %collective-permute-done.5.refs_1_ = bf16[128,640]{1,0:T(8,128)(2,1)S(1)} collective-permute-done((bf16[128,640]{1,0:T(8,128)(2,1)S(1)}, bf16[128,640]{1,0:T(8,128)(2,1)S(1)}, u32[]{:S(2)}, u32[]{:S(2)}) %collective-permute-start.5) | collective-permute-done | bytes 163872 | tf_op jit(solution)/shard_map/ppermute | solution.py:260
  38.4 6.1 %collective-permute-done.6.refs_2_ = bf16[128,640]{1,0:T(8,128)(2,1)S(1)} collective-permute-done((bf16[128,640]{1,0:T(8,128)(2,1)S(1)}, bf16[128,640]{1,0:T(8,128)(2,1)S(1)}, u32[]{:S(2)}, u32[]{:S(2)}) %collective-permute-start.6) | collective-permute-done | bytes 163872 | tf_op jit(solution)/shard_map/ppermute | solution.py:260
  44.5 0.0 collective-permute-done.7.refs_3_
  44.5 0.3 all-to-all-done
  44.7 0.0 copy-start.6
  44.8 0.0 copy-start.1
  44.8 2.8 %attend.1 = bf16[16,144,128]{2,1,0:T(8,128)(2,1)} custom-call(f32[2,512]{1,0:T(2,128)S(1)} %get-tuple-element.7.bias_ref, bf16[512,1152]{1,0:T(8,128)(2,1)S(1)} %bitcast.12, bf16[128,640]{1,0:T(8,128)(2,1)S(1)} %get-tuple-element.10.refs_0_, bf16[128,640]{1,0:T(8,128)(2,1)S(1)} %collective-permute-done.5.refs_1_, ...), custom_call_target="tpu_custom_call" | custom-call | tf_op jit(solution)/shard_map/attend/pallas_call | solution.py:263
  47.5 6.8 %all-to-all-start.1 = ((bf16[16,144,128]{2,1,0:T(8,128)(2,1)}), bf16[16,144,128]{2,1,0:T(8,128)(2,1)S(1)}, u32[]{:S(2)}, u32[]{:S(2)}) async-start(bf16[16,144,128]{2,1,0:T(8,128)(2,1)} %attend.1), calls=%async_computation.1 | async-start | bytes 1179648 | tf_op jit(solution)/shard_map/all_to_all | solution.py:277
  54.3 0.0 copy-done.6
  54.3 10.4 %all-to-all-done.1.got_ref = bf16[16,144,128]{2,1,0:T(8,128)(2,1)S(1)} async-done(((bf16[16,144,128]{2,1,0:T(8,128)(2,1)}), bf16[16,144,128]{2,1,0:T(8,128)(2,1)S(1)}, u32[]{:S(2)}, u32[]{:S(2)}) %all-to-all-start.1) | async-done | bytes 589856 | tf_op jit(solution)/shard_map/all_to_all | solution.py:277
  64.8 0.0 copy-done.1
  64.8 1.4 %merge.1 = bf16[64,128]{1,0:T(8,128)(2,1)} custom-call(bf16[16,144,128]{2,1,0:T(8,128)(2,1)S(1)} %all-to-all-done.1.got_ref, bf16[2,32,640]{2,1,0:T(8,128)(2,1)S(1)} %get-tuple-element.8.query_ref, bf16[8,576]{1,0:T(8,128)(2,1)S(1)} %reshape.18.new_ref, bf16[8,512,128]{2,1,0:T(8,128)(2,1)S(1)} %copy-done.1), custom_call_target="tpu_custom_call" | custom-call | tf_op jit(solution)/shard_map/merge/pallas_call | solution.py:279
  (6 shorter events, 0.1 us)
Async XLA Ops:
  0.0 3.2 %collective-permute-start.1 = (bf16[16,64,576]{2,1,0:T(8,128)(2,1)}, bf16[16,64,576]{2,1,0:T(8,128)(2,1)S(1)}, u32[]{:S(2)}, u32[]{:S(2)}) collective-permute-start(bf16[16,64,576]{2,1,0:T(8,128)(2,1)} %bitcast.14), channel_id=1, source_target_pairs={{0,128},{128,0},{1,129},{129,1},{2,130},{130,2},{3,131},{131,3},{4... | collective-permute-start | bytes 3538952 | tf_op jit(solution)/shard_map/ppermute | solution.py:216
  0.0 3.2 %collective-permute-start = (s32[1,16]{1,0:T(1,128)}, s32[1,16]{1,0:T(1,128)S(1)}, u32[]{:S(2)}, u32[]{:S(2)}) collective-permute-start(s32[1,16]{1,0:T(1,128)} %bitcast.15), channel_id=1, source_target_pairs={{0,128},{128,0},{1,129},{129,1},{2,130},{130,2},{3,131},{131,3},{4... | collective-permute-start | bytes 200 | tf_op jit(solution)/shard_map/ppermute | solution.py:217
  3.2 0.7 copy-start.3
  5.7 9.8 %copy-start = (bf16[8,128,512]{2,1,0:T(8,128)(2,1)S(1)}, bf16[8,128,512]{2,1,0:T(8,128)(2,1)}, u32[]{:S(2)}) copy-start(bf16[8,128,512]{2,1,0:T(8,128)(2,1)} %w_ref.2) | copy-start | bytes 3145732
  5.7 9.8 %copy-start.2 = (bf16[1,2,4,8,192]{4,3,2,1,0:T(8,128)(2,1)S(1)}, bf16[1,2,4,8,192]{4,3,2,1,0:T(8,128)(2,1)}, u32[]{:S(2)}) copy-start(bf16[1,2,4,8,192]{4,3,2,1,0:T(8,128)(2,1)} %param.12) | copy-start | bytes 73732
  5.7 9.8 %copy-start.4 = (s32[1,16]{1,0:T(1,128)S(1)}, s32[1,16]{1,0:T(1,128)}, u32[]{:S(2)}) copy-start(s32[1,16]{1,0:T(1,128)} %request_ref.3) | copy-start | bytes 196
  5.8 9.8 %copy-start.5 = (s32[2,16]{1,0:T(2,128)S(1)}, s32[2,16]{1,0:T(2,128)}, u32[]{:S(2)}) copy-start(s32[2,16]{1,0:T(2,128)} %lengths_ref.1) | copy-start | bytes 388
  5.8 39.0 %all-to-all-start = ((bf16[16,32,1152]{2,1,0:T(8,128)(2,1)}), bf16[16,32,1152]{2,1,0:T(8,128)(2,1)S(1)}, u32[]{:S(2)}, u32[]{:S(2)}) async-start(bf16[16,32,1152]{2,1,0:T(8,128)(2,1)} %pack.1), calls=%async_computation | async-start | bytes 2359296 | tf_op jit(solution)/shard_map/all_to_all | solution.py:233
  16.4 4.8 %collective-permute-start.2 = (bf16[2,32,640]{2,1,0:T(8,128)(2,1)S(1)}, bf16[2,32,640]{2,1,0:T(8,128)(2,1)S(1)}, u32[]{:S(2)}, u32[]{:S(2)}) collective-permute-start(bf16[2,32,640]{2,1,0:T(8,128)(2,1)S(1)} %get-tuple-element.8.query_ref), channel_id=1, source_target_pairs={{0,8},{8,0},{16,24},{24,16},{32,40},{40,32},{48,56},{56,48},{64,72... | collective-permute-start | bytes 245768 | tf_op jit(solution)/shard_map/ppermute | solution.py:251
  18.1 6.6 %collective-permute-start.3 = (bf16[2,32,640]{2,1,0:T(8,128)(2,1)S(1)}, bf16[2,32,640]{2,1,0:T(8,128)(2,1)S(1)}, u32[]{:S(2)}, u32[]{:S(2)}) collective-permute-start(bf16[2,32,640]{2,1,0:T(8,128)(2,1)S(1)} %get-tuple-element.8.query_ref), channel_id=1, source_target_pairs={{0,16},{8,24},{16,0},{24,8},{32,48},{40,56},{48,32},{56,40},{64,80... | collective-permute-start | bytes 245768 | tf_op jit(solution)/shard_map/ppermute | solution.py:251
  21.0 5.7 %collective-permute-start.4 = (bf16[2,32,640]{2,1,0:T(8,128)(2,1)S(1)}, bf16[2,32,640]{2,1,0:T(8,128)(2,1)S(1)}, u32[]{:S(2)}, u32[]{:S(2)}) collective-permute-start(bf16[2,32,640]{2,1,0:T(8,128)(2,1)S(1)} %get-tuple-element.8.query_ref), channel_id=1, source_target_pairs={{0,24},{8,16},{16,8},{24,0},{32,56},{40,48},{48,40},{56,32},{64,88... | collective-permute-start | bytes 245768 | tf_op jit(solution)/shard_map/ppermute | solution.py:251
  26.7 11.7 %collective-permute-start.5 = (bf16[128,640]{1,0:T(8,128)(2,1)S(1)}, bf16[128,640]{1,0:T(8,128)(2,1)S(1)}, u32[]{:S(2)}, u32[]{:S(2)}) collective-permute-start(bf16[128,640]{1,0:T(8,128)(2,1)S(1)} %get-tuple-element.9), channel_id=1, source_target_pairs={{0,32},{8,40},{16,48},{24,56},{32,64},{40,72},{48,80},{56,88},{64,... | collective-permute-start | bytes 491528 | tf_op jit(solution)/shard_map/ppermute | solution.py:260
  28.2 16.3 %collective-permute-start.6 = (bf16[128,640]{1,0:T(8,128)(2,1)S(1)}, bf16[128,640]{1,0:T(8,128)(2,1)S(1)}, u32[]{:S(2)}, u32[]{:S(2)}) collective-permute-start(bf16[128,640]{1,0:T(8,128)(2,1)S(1)} %get-tuple-element.10.refs_0_), channel_id=1, source_target_pairs={{0,64},{8,72},{16,80},{24,88},{32,96},{40,104},{48,112},{56,120},{... | collective-permute-start | bytes 491528 | tf_op jit(solution)/shard_map/ppermute | solution.py:260
  30.9 13.5 %collective-permute-start.7 = (bf16[128,640]{1,0:T(8,128)(2,1)S(1)}, bf16[128,640]{1,0:T(8,128)(2,1)S(1)}, u32[]{:S(2)}, u32[]{:S(2)}) collective-permute-start(bf16[128,640]{1,0:T(8,128)(2,1)S(1)} %get-tuple-element.9), channel_id=1, source_target_pairs={{0,96},{8,104},{16,112},{24,120},{32,0},{40,8},{48,16},{56,24},{64... | collective-permute-start | bytes 491528 | tf_op jit(solution)/shard_map/ppermute | solution.py:260
  44.7 9.6 %copy-start.6 = (bf16[1,2,4,576]{3,2,1,0:T(4,128)(2,1)S(1)}, bf16[1,2,4,576]{3,2,1,0:T(4,128)(2,1)}, u32[]{:S(2)}) copy-start(bf16[1,2,4,576]{3,2,1,0:T(4,128)(2,1)} %param.13) | copy-start | bytes 27652
  44.8 20.0 %copy-start.1 = (bf16[8,512,128]{2,1,0:T(8,128)(2,1)S(1)}, bf16[8,512,128]{2,1,0:T(8,128)(2,1)}, u32[]{:S(2)}) copy-start(bf16[8,512,128]{2,1,0:T(8,128)(2,1)} %w_ref.3) | copy-start | bytes 3145732
  47.5 17.2 %all-to-all-start.1 = ((bf16[16,144,128]{2,1,0:T(8,128)(2,1)}), bf16[16,144,128]{2,1,0:T(8,128)(2,1)S(1)}, u32[]{:S(2)}, u32[]{:S(2)}) async-start(bf16[16,144,128]{2,1,0:T(8,128)(2,1)} %attend.1), calls=%async_computation.1 | async-start | bytes 1179648 | tf_op jit(solution)/shard_map/all_to_all | solution.py:277

commit v3 on v2

--- a/solution.py
+++ b/solution.py
@@ -142,21 +142,44 @@
         send.wait()
 
 
-def merge_kernel(scale2, got_ref, query_ref, new_ref, w_ref, out_ref):
+def fresh_kernel(scale2, query_ref, new_ref, best_ref, sum_ref, value_ref):
+    rows, width = query_ref.shape[1:]
+    latent = width - LANES
+    count = new_ref.shape[0] // 2
+    heads = rows // count
+    token = lax.broadcasted_iota(jnp.int32, (rows, count), 0) // heads
+    causal = lax.broadcasted_iota(jnp.int32, (rows, count), 1) <= token
+    for r in range(2):
+        part = slice(r * rows, (r + 1) * rows)
+        mine = new_ref[...].astype(jnp.float32)[r * count : (r + 1) * count]
+        new_lat, rope = mine[:, :latent], mine[:, latent:]
+        keys = jnp.concatenate([mine, jnp.zeros_like(rope)], axis=1).astype(jnp.bfloat16)
+        scores = lax.dot_general(query_ref[r], keys, NT, preferred_element_type=jnp.float32)
+        scores = jnp.where(causal, scores * scale2, FILL_LOW)
+        best = jnp.max(scores, axis=1, keepdims=True)
+        weights = jnp.exp2(scores - best)
+        best_ref[part] = jnp.broadcast_to(best, (rows, LANES))
+        sum_ref[part] = jnp.broadcast_to(jnp.sum(weights, axis=1, keepdims=True), (rows, LANES))
+        weights = weights.astype(jnp.bfloat16).astype(jnp.float32)
+        value = weights[:, :1] * new_lat[:1]
+        for j in range(1, count):
+            value = value + weights[:, j : j + 1] * new_lat[j : j + 1]
+        value_ref[part] = value
+
+
+def merge_kernel(got_ref, best_ref, sum_ref, value_ref, w_ref, out_ref):
     n_seq = got_ref.shape[0]
     heads, latent, _ = w_ref.shape
-    rows = query_ref.shape[1]
+    rows = best_ref.shape[0] // 2
     chunks = latent // LANES
     tail = chunks * rows
     lane = lax.broadcasted_iota(jnp.int32, (rows, LANES), 1)
     base = PARTS * (lax.broadcasted_iota(jnp.int32, (rows, LANES), 0) // FOLD)
     in_best = (lane >= base) & (lane < base + 3)
     in_sum = (lane >= base + 3) & (lane < base + 5)
-    count = new_ref.shape[0] // 2
-    token = lax.broadcasted_iota(jnp.int32, (rows, count), 0) // heads
-    causal = lax.broadcasted_iota(jnp.int32, (rows, count), 1) <= token
     latent_out = []
     for r in range(2):
+        part = slice(r * rows, (r + 1) * rows)
         sources = [i for i in range(n_seq) if i // N_NEAR % 2 == r]
         bests, sums = [], []
         for i in sources:
@@ -164,30 +187,22 @@
             stats = jnp.concatenate([stats] * (rows // FOLD), axis=0)
             bests.append(jnp.sum(jnp.where(in_best, stats, 0.0), axis=1, keepdims=True))
             sums.append(jnp.sum(jnp.where(in_sum, stats, 0.0), axis=1, keepdims=True))
-        new_keys = new_ref[...].astype(jnp.float32)[r * count : (r + 1) * count]
-        new_lat, rope = new_keys[:, :latent], new_keys[:, latent:]
-        keys = jnp.concatenate([new_keys, jnp.zeros_like(rope)], axis=1).astype(jnp.bfloat16)
-        new_scores = lax.dot_general(query_ref[r], keys, NT, preferred_element_type=jnp.float32)
-        new_scores = jnp.where(causal, new_scores * scale2, FILL_LOW)
-        best = jnp.max(new_scores, axis=1, keepdims=True)
+        fresh_best = best_ref[part]
+        best = fresh_best
         for one in bests:
             best = jnp.maximum(best, one)
-        new_weights = jnp.where(causal, jnp.exp2(new_scores - best), 0.0)
-        total = jnp.sum(new_weights, axis=1, keepdims=True)
-        new_weights = new_weights.astype(jnp.bfloat16).astype(jnp.float32)
+        fresh_factor = jnp.exp2(fresh_best - best)
         factors = [jnp.exp2(one - best) for one in bests]
+        total = fresh_factor * sum_ref[part]
         for factor, one in zip(factors, sums):
             total = total + factor * one
+        inverse = 1.0 / total
         pieces = []
         for c in range(chunks):
-            value = jnp.zeros((rows, LANES), jnp.float32)
-            for j in range(count):
-                value = value + (
-                    new_weights[:, j : j + 1] * new_lat[j : j + 1, c * LANES : (c + 1) * LANES]
-                )
+            value = fresh_factor * value_ref[part, c * LANES : (c + 1) * LANES]
             for factor, i in zip(factors, sources):
                 value = value + factor * got_ref[i, c * rows : (c + 1) * rows].astype(jnp.float32)
-            pieces.append((value / total).astype(jnp.bfloat16))
+            pieces.append((value * inverse).astype(jnp.bfloat16))
         latent_out.append(jnp.concatenate(pieces, axis=1))
     latent_out = jnp.concatenate(latent_out, axis=0)
     head_of = lax.broadcasted_iota(jnp.int32, out_ref.shape, 0) % heads
@@ -215,6 +230,7 @@
 
     pool = lax.ppermute(latent_pool[0], "grp", swap)
     table = lax.ppermute(block_table.reshape(1, -1), "grp", swap)
+    order = jnp.clip(row_request, 0, row_request.shape[1] - 1)
     packed_shape = (2 * n_row, page_rows // 2, 2 * latent_dim + LANES)
     packed = pl.pallas_call(
         pack_kernel,
@@ -224,7 +240,7 @@
         scratch_shapes=[pltpu.VMEM(packed_shape, bf16), pltpu.SemaphoreType.DMA((2 * n_row,))],
         compiler_params=params(16),
         name="pack",
-    )(row_request, table, pool)
+    )(order, table, pool)
     pairs = [
         [(base + pair * N_NEAR) * n_row + row for pair in range(2) for row in range(n_row)]
         for base in range(n_seq)
@@ -276,14 +292,25 @@
     )(bias, got_cache.reshape(keys, -1), *all_query)
     got = lax.all_to_all(message, "seq", 0, 0, tiled=True)
 
+    fresh = pl.pallas_call(
+        functools.partial(fresh_kernel, scale2),
+        out_shape=[
+            jax.ShapeDtypeStruct((block_rows, width), jnp.float32)
+            for width in (LANES, LANES, latent_dim)
+        ],
+        in_specs=[vmem()] * 2,
+        out_specs=[vmem()] * 3,
+        compiler_params=params(16),
+        name="fresh",
+    )(own_query, new_latent.reshape(rows_dev * n_new, lat_width))
     result = pl.pallas_call(
-        functools.partial(merge_kernel, scale2),
+        merge_kernel,
         out_shape=jax.ShapeDtypeStruct((block_rows, value_dim), bf16),
-        in_specs=[vmem()] * 4,
+        in_specs=[vmem()] * 5,
         out_specs=vmem(),
         compiler_params=params(16),
         name="merge",
-    )(got, own_query, new_latent.reshape(rows_dev * n_new, lat_width), w_uv)
+    )(got, *fresh, w_uv)
     return result.reshape(1, rows_dev, n_new, head_dev, value_dim)
 
 

time: 66.5 us -> 65.5 us (0.985)
  waiting for transfers between devices: 31.2 us -> 30.1 us
    pallas_call x1 -> x2, Pallas kernels: 1.44 us -> 1.55 us  [the longest x1 1.15 us: per_device(): pl.pallas_call(merge_kernel, out_shape=jax.ShapeDtypeStruct((block_rows,...]
  transfers between devices with their start and end apart: 10 -> 10, of which waited for: 7 -> 7; matrix products, arithmetic and copies ran while one was open for 0% -> 1% of each run, Pallas kernels for 1% -> 2%
where the time goes in v3:
time: 65.5 us; the launch traced here: 65.3 us
  waiting for transfers between devices  30.1 us (46%)
  starting transfers between devices  27.1 us (41%)
  Pallas kernels  7 us (11%)
  other arithmetic  0.73 us (1%)
    ppermute x3, waiting for transfers between devices, per_device(): all_query.append(lax.ppermute(other if j % 2 else same, 'seq', route))  12.4 us
    all_to_all x1, waiting for transfers between devices, per_device(): got = lax.all_to_all(message, 'seq', 0, 0, tiled=True)  10 us
    all_to_all x1, starting transfers between devices, per_device(): lax.all_to_all(packed, ('seq', 'row'), 0, 0, axis_index_groups=pairs, til...  9.66 us
    all_to_all x1, starting transfers between devices, per_device(): got = lax.all_to_all(message, 'seq', 0, 0, tiled=True)  6.76 us
    ppermute x3, starting transfers between devices, per_device(): all_query.append(lax.ppermute(other if j % 2 else same, 'seq', route))  5.44 us
    ppermute x3, waiting for transfers between devices, per_device(): lax.ppermute(own_query, 'seq', [(s, s ^ k) for s in range(n_seq)])  5.38 us
    ppermute x3, starting transfers between devices, per_device(): lax.ppermute(own_query, 'seq', [(s, s ^ k) for s in range(n_seq)])  4.79 us
    pallas_call x1, Pallas kernels, per_device(): pl.pallas_call(functools.partial(attend_kernel, scale2), out_shape=jax.Sh...  2.78 us
  transfers between devices with their start and end apart: 10, of which 7 were waited for; matrix products, arithmetic and copies ran while one was open for 1% of the time, Pallas kernels for 2%

profile of v3, /device:TPU:32, one launch (start us, length us, event | category | flops | bytes accessed | tf_op | source)
XLA Modules:
  0.0 65.3 jit_solution(208356332180269680)
XLA Ops:
  0.0 0.0 collective-permute-start.1
  0.0 0.5 collective-permute-start
  0.5 0.7 %broadcast_clamp_fusion.request_ref = s32[1,16]{1,0:T(1,128)S(1)} fusion(s32[1,16]{1,0:T(1,128)} %request_ref.1), kind=kLoop, calls=%fused_computation.7 | loop fusion | flops 16 | bytes 128 | tf_op jit(solution)/shard_map/jit(clip)/min | solution.py:233
  1.2 2.1 %collective-permute-done.table_ref = s32[1,16]{1,0:T(1,128)S(1)} collective-permute-done((s32[1,16]{1,0:T(1,128)}, s32[1,16]{1,0:T(1,128)S(1)}, u32[]{:S(2)}, u32[]{:S(2)}) %collective-permute-start) | collective-permute-done | bytes 96 | tf_op jit(solution)/shard_map/ppermute | solution.py:232
  3.2 0.0 collective-permute-done.1.pool_ref
  3.2 1.8 %pack.1 = bf16[16,32,1152]{2,1,0:T(8,128)(2,1)} custom-call(s32[1,16]{1,0:T(1,128)S(1)} %broadcast_clamp_fusion.request_ref, s32[1,16]{1,0:T(1,128)S(1)} %collective-permute-done.table_ref, bf16[16,64,576]{2,1,0:T(8,128)(2,1)S(1)} %collective-permute-done.1.pool_ref), custom_call_target="tpu_custom_call" | custom-call | tf_op jit(solution)/shard_map/pack/pallas_call | solution.py:235
  5.1 0.0 copy-start.1
  5.1 0.0 copy-start.2
  5.1 0.0 copy-start.3
  5.1 0.0 copy-start.4
  5.1 9.7 %all-to-all-start = ((bf16[16,32,1152]{2,1,0:T(8,128)(2,1)}), bf16[16,32,1152]{2,1,0:T(8,128)(2,1)S(1)}, u32[]{:S(2)}, u32[]{:S(2)}) async-start(bf16[16,32,1152]{2,1,0:T(8,128)(2,1)} %pack.1), calls=%async_computation | async-start | bytes 2359296 | tf_op jit(solution)/shard_map/all_to_all | solution.py:249
  14.8 0.1 pad_add_fusion.place_ref
  14.9 0.0 copy-done.1
  14.9 0.0 copy-done.2
  14.9 0.0 copy-done.3
  14.9 0.0 copy-done.4
  14.9 0.9 %query.1 = (bf16[2,32,640]{2,1,0:T(8,128)(2,1)S(1)}, f32[2,512]{1,0:T(2,128)S(1)}) custom-call(s32[3]{0:T(128)S(1)} %pad_add_fusion.place_ref, s32[2,16]{1,0:T(2,128)S(1)} %copy-done.3, s32[1,16]{1,0:T(1,128)S(1)} %copy-done.4, bf16[64,192]{1,0:T(8,128)(2,1)S(1)} %bitcast.13, bf16[8,128,512]{2,1,0:T(8,128)(2,1)S(1)} %copy-done.1), custom_call_target="tpu_custom_call" | custom-call | tf_op jit(solution)/shard_map/query/pallas_call | solution.py:254
  15.7 1.7 %collective-permute-start.2 = (bf16[2,32,640]{2,1,0:T(8,128)(2,1)S(1)}, bf16[2,32,640]{2,1,0:T(8,128)(2,1)S(1)}, u32[]{:S(2)}, u32[]{:S(2)}) collective-permute-start(bf16[2,32,640]{2,1,0:T(8,128)(2,1)S(1)} %get-tuple-element.11.query_ref), channel_id=1, source_target_pairs={{0,8},{8,0},{16,24},{24,16},{32,40},{40,32},{48,56},{56,48},{64,72... | collective-permute-start | bytes 245768 | tf_op jit(solution)/shard_map/ppermute | solution.py:267
  17.4 2.9 %collective-permute-start.3 = (bf16[2,32,640]{2,1,0:T(8,128)(2,1)S(1)}, bf16[2,32,640]{2,1,0:T(8,128)(2,1)S(1)}, u32[]{:S(2)}, u32[]{:S(2)}) collective-permute-start(bf16[2,32,640]{2,1,0:T(8,128)(2,1)S(1)} %get-tuple-element.11.query_ref), channel_id=1, source_target_pairs={{0,16},{8,24},{16,0},{24,8},{32,48},{40,56},{48,32},{56,40},{64,80... | collective-permute-start | bytes 245768 | tf_op jit(solution)/shard_map/ppermute | solution.py:267
  20.3 0.2 collective-permute-start.4
  20.5 0.0 collective-permute-done.2
  20.6 3.5 %collective-permute-done.3 = bf16[2,32,640]{2,1,0:T(8,128)(2,1)S(1)} collective-permute-done((bf16[2,32,640]{2,1,0:T(8,128)(2,1)S(1)}, bf16[2,32,640]{2,1,0:T(8,128)(2,1)S(1)}, u32[]{:S(2)}, u32[]{:S(2)}) %collective-permute-start.3) | collective-permute-done | bytes 81952 | tf_op jit(solution)/shard_map/ppermute | solution.py:267
  24.1 1.9 %collective-permute-done.4 = bf16[2,32,640]{2,1,0:T(8,128)(2,1)S(1)} collective-permute-done((bf16[2,32,640]{2,1,0:T(8,128)(2,1)S(1)}, bf16[2,32,640]{2,1,0:T(8,128)(2,1)S(1)}, u32[]{:S(2)}, u32[]{:S(2)}) %collective-permute-start.4) | collective-permute-done | bytes 81952 | tf_op jit(solution)/shard_map/ppermute | solution.py:267
  26.0 1.5 %collective-permute-start.5 = (bf16[128,640]{1,0:T(8,128)(2,1)S(1)}, bf16[128,640]{1,0:T(8,128)(2,1)S(1)}, u32[]{:S(2)}, u32[]{:S(2)}) collective-permute-start(bf16[128,640]{1,0:T(8,128)(2,1)S(1)} %get-tuple-element.15), channel_id=1, source_target_pairs={{0,32},{8,40},{16,48},{24,56},{32,64},{40,72},{48,80},{56,88},{64,... | collective-permute-start | bytes 491528 | tf_op jit(solution)/shard_map/ppermute | solution.py:276
  27.6 2.7 %collective-permute-start.6 = (bf16[128,640]{1,0:T(8,128)(2,1)S(1)}, bf16[128,640]{1,0:T(8,128)(2,1)S(1)}, u32[]{:S(2)}, u32[]{:S(2)}) collective-permute-start(bf16[128,640]{1,0:T(8,128)(2,1)S(1)} %get-tuple-element.16.refs_0_), channel_id=1, source_target_pairs={{0,64},{8,72},{16,80},{24,88},{32,96},{40,104},{48,112},{56,120},{... | collective-permute-start | bytes 491528 | tf_op jit(solution)/shard_map/ppermute | solution.py:276
  30.3 1.2 %collective-permute-start.7 = (bf16[128,640]{1,0:T(8,128)(2,1)S(1)}, bf16[128,640]{1,0:T(8,128)(2,1)S(1)}, u32[]{:S(2)}, u32[]{:S(2)}) collective-permute-start(bf16[128,640]{1,0:T(8,128)(2,1)S(1)} %get-tuple-element.15), channel_id=1, source_target_pairs={{0,96},{8,104},{16,112},{24,120},{32,0},{40,8},{48,16},{56,24},{64... | collective-permute-start | bytes 491528 | tf_op jit(solution)/shard_map/ppermute | solution.py:276
  31.5 6.3 %collective-permute-done.5.refs_1_ = bf16[128,640]{1,0:T(8,128)(2,1)S(1)} collective-permute-done((bf16[128,640]{1,0:T(8,128)(2,1)S(1)}, bf16[128,640]{1,0:T(8,128)(2,1)S(1)}, u32[]{:S(2)}, u32[]{:S(2)}) %collective-permute-start.5) | collective-permute-done | bytes 163872 | tf_op jit(solution)/shard_map/ppermute | solution.py:276
  37.7 6.1 %collective-permute-done.6.refs_2_ = bf16[128,640]{1,0:T(8,128)(2,1)S(1)} collective-permute-done((bf16[128,640]{1,0:T(8,128)(2,1)S(1)}, bf16[128,640]{1,0:T(8,128)(2,1)S(1)}, u32[]{:S(2)}, u32[]{:S(2)}) %collective-permute-start.6) | collective-permute-done | bytes 163872 | tf_op jit(solution)/shard_map/ppermute | solution.py:276
  43.8 0.0 collective-permute-done.7.refs_3_
  43.8 0.3 all-to-all-done
  44.1 0.0 copy-start.5
  44.1 0.0 copy-start
  44.1 2.8 %attend.1 = bf16[16,144,128]{2,1,0:T(8,128)(2,1)} custom-call(f32[2,512]{1,0:T(2,128)S(1)} %get-tuple-element.10.bias_ref, bf16[512,1152]{1,0:T(8,128)(2,1)S(1)} %bitcast.12, bf16[128,640]{1,0:T(8,128)(2,1)S(1)} %get-tuple-element.16.refs_0_, bf16[128,640]{1,0:T(8,128)(2,1)S(1)} %collective-permute-done.5.refs_1_, ...), custom_call_target="tpu_custom_call" | custom-call | tf_op jit(solution)/shard_map/attend/pallas_call | solution.py:279
  46.9 6.8 %all-to-all-start.1 = ((bf16[16,144,128]{2,1,0:T(8,128)(2,1)}), bf16[16,144,128]{2,1,0:T(8,128)(2,1)S(1)}, u32[]{:S(2)}, u32[]{:S(2)}) async-start(bf16[16,144,128]{2,1,0:T(8,128)(2,1)} %attend.1), calls=%async_computation.1 | async-start | bytes 1179648 | tf_op jit(solution)/shard_map/all_to_all | solution.py:293
  53.7 0.0 copy-done.5
  53.7 0.4 fresh.1
  54.1 10.0 %all-to-all-done.1.got_ref = bf16[16,144,128]{2,1,0:T(8,128)(2,1)S(1)} async-done(((bf16[16,144,128]{2,1,0:T(8,128)(2,1)}), bf16[16,144,128]{2,1,0:T(8,128)(2,1)S(1)}, u32[]{:S(2)}, u32[]{:S(2)}) %all-to-all-start.1) | async-done | bytes 589856 | tf_op jit(solution)/shard_map/all_to_all | solution.py:293
  64.1 0.0 copy-done
  64.1 1.2 %merge.1 = bf16[64,128]{1,0:T(8,128)(2,1)} custom-call(bf16[16,144,128]{2,1,0:T(8,128)(2,1)S(1)} %all-to-all-done.1.got_ref, f32[64,128]{1,0:T(8,128)S(1)} %get-tuple-element.12.best_ref, f32[64,128]{1,0:T(8,128)S(1)} %get-tuple-element.13.sum_ref, f32[64,512]{1,0:T(8,128)S(1)} %get-tuple-element.14.value_ref, bf16[8,512,128]{2,1,0:T(8,128)(2,1)S(1)} %copy-done), custom_call_target="tpu_custom_call" | custom-call | tf_op jit(solution)/shard_map/merge/pallas_call | solution.py:306
  (6 shorter events, 0.1 us)
Async XLA Ops:
  0.0 3.2 %collective-permute-start.1 = (bf16[16,64,576]{2,1,0:T(8,128)(2,1)}, bf16[16,64,576]{2,1,0:T(8,128)(2,1)S(1)}, u32[]{:S(2)}, u32[]{:S(2)}) collective-permute-start(bf16[16,64,576]{2,1,0:T(8,128)(2,1)} %bitcast.14), channel_id=1, source_target_pairs={{0,128},{128,0},{1,129},{129,1},{2,130},{130,2},{3,131},{131,3},{4... | collective-permute-start | bytes 3538952 | tf_op jit(solution)/shard_map/ppermute | solution.py:231
  0.0 3.2 %collective-permute-start = (s32[1,16]{1,0:T(1,128)}, s32[1,16]{1,0:T(1,128)S(1)}, u32[]{:S(2)}, u32[]{:S(2)}) collective-permute-start(s32[1,16]{1,0:T(1,128)} %bitcast.15), channel_id=1, source_target_pairs={{0,128},{128,0},{1,129},{129,1},{2,130},{130,2},{3,131},{131,3},{4... | collective-permute-start | bytes 200 | tf_op jit(solution)/shard_map/ppermute | solution.py:232
  5.1 9.8 %copy-start.1 = (bf16[8,128,512]{2,1,0:T(8,128)(2,1)S(1)}, bf16[8,128,512]{2,1,0:T(8,128)(2,1)}, u32[]{:S(2)}) copy-start(bf16[8,128,512]{2,1,0:T(8,128)(2,1)} %w_ref.2) | copy-start | bytes 3145732
  5.1 9.8 %copy-start.2 = (bf16[1,2,4,8,192]{4,3,2,1,0:T(8,128)(2,1)S(1)}, bf16[1,2,4,8,192]{4,3,2,1,0:T(8,128)(2,1)}, u32[]{:S(2)}) copy-start(bf16[1,2,4,8,192]{4,3,2,1,0:T(8,128)(2,1)} %param.12) | copy-start | bytes 73732
  5.1 9.8 %copy-start.3 = (s32[2,16]{1,0:T(2,128)S(1)}, s32[2,16]{1,0:T(2,128)}, u32[]{:S(2)}) copy-start(s32[2,16]{1,0:T(2,128)} %lengths_ref.1) | copy-start | bytes 388
  5.1 9.8 %copy-start.4 = (s32[1,16]{1,0:T(1,128)S(1)}, s32[1,16]{1,0:T(1,128)}, u32[]{:S(2)}) copy-start(s32[1,16]{1,0:T(1,128)} %request_ref.1) | copy-start | bytes 196
  5.1 39.0 %all-to-all-start = ((bf16[16,32,1152]{2,1,0:T(8,128)(2,1)}), bf16[16,32,1152]{2,1,0:T(8,128)(2,1)S(1)}, u32[]{:S(2)}, u32[]{:S(2)}) async-start(bf16[16,32,1152]{2,1,0:T(8,128)(2,1)} %pack.1), calls=%async_computation | async-start | bytes 2359296 | tf_op jit(solution)/shard_map/all_to_all | solution.py:249
  15.7 4.8 %collective-permute-start.2 = (bf16[2,32,640]{2,1,0:T(8,128)(2,1)S(1)}, bf16[2,32,640]{2,1,0:T(8,128)(2,1)S(1)}, u32[]{:S(2)}, u32[]{:S(2)}) collective-permute-start(bf16[2,32,640]{2,1,0:T(8,128)(2,1)S(1)} %get-tuple-element.11.query_ref), channel_id=1, source_target_pairs={{0,8},{8,0},{16,24},{24,16},{32,40},{40,32},{48,56},{56,48},{64,72... | collective-permute-start | bytes 245768 | tf_op jit(solution)/shard_map/ppermute | solution.py:267
  17.4 6.6 %collective-permute-start.3 = (bf16[2,32,640]{2,1,0:T(8,128)(2,1)S(1)}, bf16[2,32,640]{2,1,0:T(8,128)(2,1)S(1)}, u32[]{:S(2)}, u32[]{:S(2)}) collective-permute-start(bf16[2,32,640]{2,1,0:T(8,128)(2,1)S(1)} %get-tuple-element.11.query_ref), channel_id=1, source_target_pairs={{0,16},{8,24},{16,0},{24,8},{32,48},{40,56},{48,32},{56,40},{64,80... | collective-permute-start | bytes 245768 | tf_op jit(solution)/shard_map/ppermute | solution.py:267
  20.3 5.7 %collective-permute-start.4 = (bf16[2,32,640]{2,1,0:T(8,128)(2,1)S(1)}, bf16[2,32,640]{2,1,0:T(8,128)(2,1)S(1)}, u32[]{:S(2)}, u32[]{:S(2)}) collective-permute-start(bf16[2,32,640]{2,1,0:T(8,128)(2,1)S(1)} %get-tuple-element.11.query_ref), channel_id=1, source_target_pairs={{0,24},{8,16},{16,8},{24,0},{32,56},{40,48},{48,40},{56,32},{64,88... | collective-permute-start | bytes 245768 | tf_op jit(solution)/shard_map/ppermute | solution.py:267
  26.0 11.7 %collective-permute-start.5 = (bf16[128,640]{1,0:T(8,128)(2,1)S(1)}, bf16[128,640]{1,0:T(8,128)(2,1)S(1)}, u32[]{:S(2)}, u32[]{:S(2)}) collective-permute-start(bf16[128,640]{1,0:T(8,128)(2,1)S(1)} %get-tuple-element.15), channel_id=1, source_target_pairs={{0,32},{8,40},{16,48},{24,56},{32,64},{40,72},{48,80},{56,88},{64,... | collective-permute-start | bytes 491528 | tf_op jit(solution)/shard_map/ppermute | solution.py:276
  27.6 16.3 %collective-permute-start.6 = (bf16[128,640]{1,0:T(8,128)(2,1)S(1)}, bf16[128,640]{1,0:T(8,128)(2,1)S(1)}, u32[]{:S(2)}, u32[]{:S(2)}) collective-permute-start(bf16[128,640]{1,0:T(8,128)(2,1)S(1)} %get-tuple-element.16.refs_0_), channel_id=1, source_target_pairs={{0,64},{8,72},{16,80},{24,88},{32,96},{40,104},{48,112},{56,120},{... | collective-permute-start | bytes 491528 | tf_op jit(solution)/shard_map/ppermute | solution.py:276
  30.3 13.5 %collective-permute-start.7 = (bf16[128,640]{1,0:T(8,128)(2,1)S(1)}, bf16[128,640]{1,0:T(8,128)(2,1)S(1)}, u32[]{:S(2)}, u32[]{:S(2)}) collective-permute-start(bf16[128,640]{1,0:T(8,128)(2,1)S(1)} %get-tuple-element.15), channel_id=1, source_target_pairs={{0,96},{8,104},{16,112},{24,120},{32,0},{40,8},{48,16},{56,24},{64... | collective-permute-start | bytes 491528 | tf_op jit(solution)/shard_map/ppermute | solution.py:276
  44.1 9.6 %copy-start.5 = (bf16[1,2,4,576]{3,2,1,0:T(4,128)(2,1)S(1)}, bf16[1,2,4,576]{3,2,1,0:T(4,128)(2,1)}, u32[]{:S(2)}) copy-start(bf16[1,2,4,576]{3,2,1,0:T(4,128)(2,1)} %param.13) | copy-start | bytes 27652
  44.1 20.0 %copy-start = (bf16[8,512,128]{2,1,0:T(8,128)(2,1)S(1)}, bf16[8,512,128]{2,1,0:T(8,128)(2,1)}, u32[]{:S(2)}) copy-start(bf16[8,512,128]{2,1,0:T(8,128)(2,1)} %w_ref.3) | copy-start | bytes 3145732
  46.9 17.2 %all-to-all-start.1 = ((bf16[16,144,128]{2,1,0:T(8,128)(2,1)}), bf16[16,144,128]{2,1,0:T(8,128)(2,1)S(1)}, u32[]{:S(2)}, u32[]{:S(2)}) async-start(bf16[16,144,128]{2,1,0:T(8,128)(2,1)} %attend.1), calls=%async_computation.1 | async-start | bytes 1179648 | tf_op jit(solution)/shard_map/all_to_all | solution.py:293

commit v4 on v3

--- a/solution.py
+++ b/solution.py
@@ -53,11 +53,11 @@
     n_row = request_ref.shape[1] // 2
     keys = bias_ref.shape[1]
     half_page = keys // (2 * n_row)
-    pair = seq // N_NEAR % 2
+    pair = seq % 2
     length = lengths_ref[group, request_ref[0, row * 2 + pair]]
     key_id = lax.broadcasted_iota(jnp.int32, (1, keys), 1)
     source = key_id // half_page
-    block = (seq + (source // n_row - pair) * N_NEAR) * n_row + source % n_row
+    block = (seq - pair + source // n_row) * n_row + source % n_row
     for h in range(2):
         position = block * (2 * half_page) + h * half_page + key_id % half_page
         bias_ref[h : h + 1, :] = jnp.where(position < length, 0.0, FILL_LOW)
@@ -86,7 +86,7 @@
 
 
 def attend_kernel(scale2, bias_ref, cache_ref, *refs):
-    query_refs, (out_ref, score_ref, weight_ref, send_ref, sems) = refs[:-5], refs[-5:]
+    query_refs, (out_ref, score_ref, weight_ref) = refs[:-3], refs[-3:]
     seq = lax.axis_index("seq")
     n_seq = out_ref.shape[0]
     n_far = len(query_refs)
@@ -124,22 +124,17 @@
         for j, part in enumerate(split_bf16(best * scale2, 3) + split_bf16(weight_sum, 2)):
             stats = jnp.where(lane == base + j, part, stats)
         stats = sum(stats[i * FOLD : (i + 1) * FOLD] for i in range(rows // FOLD))
-        send_ref[b, chunks * rows :, :] = stats.astype(jnp.bfloat16)
+        out_ref[owner[b], chunks * rows :, :] = stats.astype(jnp.bfloat16)
     value = jnp.dot(weight_ref[0], cache_ref[:, :latent], preferred_element_type=jnp.float32)
     value += jnp.dot(
         weight_ref[1], cache_ref[:, latent + LANES :], preferred_element_type=jnp.float32
     )
     value = value.astype(jnp.bfloat16)
-    sends = []
     for b in range(n_seq):
         for c in range(chunks):
-            send_ref[b, c * rows : (c + 1) * rows, :] = (
+            out_ref[owner[b], c * rows : (c + 1) * rows, :] = (
                 value[b * rows : (b + 1) * rows, c * LANES : (c + 1) * LANES]
             )
-        sends.append(pltpu.make_async_copy(send_ref.at[b], out_ref.at[owner[b]], sems.at[b]))
-        sends[b].start()
-    for send in sends:
-        send.wait()
 
 
 def fresh_kernel(scale2, query_ref, new_ref, best_ref, sum_ref, value_ref):
@@ -180,7 +175,7 @@
     latent_out = []
     for r in range(2):
         part = slice(r * rows, (r + 1) * rows)
-        sources = [i for i in range(n_seq) if i // N_NEAR % 2 == r]
+        sources = range(r, n_seq, 2)
         bests, sums = [], []
         for i in sources:
             stats = got_ref[i, tail:, :].astype(jnp.float32)
@@ -242,9 +237,8 @@
         name="pack",
     )(order, table, pool)
     pairs = [
-        [(base + pair * N_NEAR) * n_row + row for pair in range(2) for row in range(n_row)]
-        for base in range(n_seq)
-        if base // N_NEAR % 2 == 0
+        [(base + pair) * n_row + row for pair in range(2) for row in range(n_row)]
+        for base in range(0, n_seq, 2)
     ]
     got_cache = lax.all_to_all(
         packed, ("seq", "row"), 0, 0, axis_index_groups=pairs, tiled=True
@@ -262,35 +256,19 @@
         compiler_params=params(16),
         name="query",
     )(place, lengths, row_request, queries.reshape(block_rows, query_width), w_uk)
-    near = [own_query]
+    pair = lax.axis_index("seq") % 2
+    same, other = (
+        lax.dynamic_index_in_dim(own_query, one, 0, keepdims=False) for one in (pair, 1 - pair)
+    )
+    near = [same]
     for k in range(1, N_NEAR):
-        near.append(lax.ppermute(own_query, "seq", [(s, s ^ k) for s in range(n_seq)]))
-    near_query = jnp.concatenate(near, axis=1)
-    pair = lax.axis_index("seq") // N_NEAR % 2
-    same, other = (
-        lax.dynamic_index_in_dim(near_query, one, 0, keepdims=False) for one in (pair, 1 - pair)
-    )
-    all_query = [same]
+        route = [(s, s ^ k) for s in range(n_seq)]
+        near.append(lax.ppermute(other if k % 2 else same, "seq", route))
+    near_query = jnp.concatenate(near, axis=0)
+    all_query = [near_query]
     for j in range(1, n_seq // N_NEAR):
         route = [(s, (s + j * N_NEAR) % n_seq) for s in range(n_seq)]
-        all_query.append(lax.ppermute(other if j % 2 else same, "seq", route))
-
-    send_shape = (n_seq, half_rows * latent_dim // LANES + FOLD, LANES)
-    message = pl.pallas_call(
-        functools.partial(attend_kernel, scale2),
-        out_shape=jax.ShapeDtypeStruct(send_shape, bf16),
-        in_specs=[vmem()] * (2 + len(all_query)),
-        out_specs=pl.BlockSpec(memory_space=pl.ANY),
-        scratch_shapes=[
-            pltpu.VMEM((2, n_seq * half_rows, keys), jnp.float32),
-            pltpu.VMEM((2, n_seq * half_rows, keys), bf16),
-            pltpu.VMEM(send_shape, bf16),
-            pltpu.SemaphoreType.DMA((n_seq,)),
-        ],
-        compiler_params=params(32),
-        name="attend",
-    )(bias, got_cache.reshape(keys, -1), *all_query)
-    got = lax.all_to_all(message, "seq", 0, 0, tiled=True)
+        all_query.append(lax.ppermute(near_query, "seq", route))
 
     fresh = pl.pallas_call(
         functools.partial(fresh_kernel, scale2),
@@ -303,6 +281,23 @@
         compiler_params=params(16),
         name="fresh",
     )(own_query, new_latent.reshape(rows_dev * n_new, lat_width))
+    all_query, fresh = lax.optimization_barrier((all_query, fresh))
+
+    send_shape = (n_seq, half_rows * latent_dim // LANES + FOLD, LANES)
+    message = pl.pallas_call(
+        functools.partial(attend_kernel, scale2),
+        out_shape=jax.ShapeDtypeStruct(send_shape, bf16),
+        in_specs=[vmem()] * (2 + len(all_query)),
+        out_specs=vmem(),
+        scratch_shapes=[
+            pltpu.VMEM((2, n_seq * half_rows, keys), jnp.float32),
+            pltpu.VMEM((2, n_seq * half_rows, keys), bf16),
+        ],
+        compiler_params=params(32),
+        name="attend",
+    )(bias, got_cache.reshape(keys, -1), *all_query)
+    got = lax.all_to_all(message, "seq", 0, 0, tiled=True)
+
     result = pl.pallas_call(
         merge_kernel,
         out_shape=jax.ShapeDtypeStruct((block_rows, value_dim), bf16),

time: 65.5 us -> 64.5 us (0.985)
  blocking collectives: 0 us -> 17 us
  waiting for transfers between devices: 30.1 us -> 20 us
  starting transfers between devices: 27.1 us -> 20.2 us
  Pallas kernels: 7 us -> 6.16 us
    all_to_all x0 -> x1, blocking collectives: none -> 17 us  [per_device(): got = lax.all_to_all(message, 'seq', 0, 0, tiled=True)]
    all_to_all x1 -> x0, waiting for transfers between devices: 10 us -> none  [per_device(): got = lax.all_to_all(message, 'seq', 0, 0, tiled=True)]
    ppermute x6, waiting for transfers between devices: 17.8 us -> 8.69 us  [the longest x3 4.8 us: per_device(): near.append(lax.ppermute(other if k % 2 else same, 'seq', route))]
    all_to_all x1, waiting for transfers between devices: 0.26 us -> 9.25 us  [per_device(): lax.all_to_all(packed, ('seq', 'row'), 0, 0, axis_index_groups=pairs, til...]
    all_to_all x1 -> x0, starting transfers between devices: 6.76 us -> none  [per_device(): got = lax.all_to_all(message, 'seq', 0, 0, tiled=True)]
    pallas_call x1, Pallas kernels: 2.78 us -> 1.93 us  [per_device(): pl.pallas_call(functools.partial(attend_kernel, scale2), out_shape=jax.Sh...]
  transfers between devices with their start and end apart: 10 -> 9, of which waited for: 7 -> 6; matrix products, arithmetic and copies ran while one was open for 1% -> 1% of each run, Pallas kernels for 2% -> 2%
where the time goes in v4:
time: 64.5 us; the launch traced here: 64.3 us
  starting transfers between devices  20.2 us (31%)
  waiting for transfers between devices  20 us (31%)
  blocking collectives  17 us (26%)
  Pallas kernels  6.16 us (10%)
  other arithmetic  0.75 us (1%)
    all_to_all x1, blocking collectives, per_device(): got = lax.all_to_all(message, 'seq', 0, 0, tiled=True)  17 us
    all_to_all x1, starting transfers between devices, per_device(): lax.all_to_all(packed, ('seq', 'row'), 0, 0, axis_index_groups=pairs, til...  9.74 us
    all_to_all x1, waiting for transfers between devices, per_device(): lax.all_to_all(packed, ('seq', 'row'), 0, 0, axis_index_groups=pairs, til...  9.25 us
    ppermute x3, starting transfers between devices, per_device(): all_query.append(lax.ppermute(near_query, 'seq', route))  5.73 us
    ppermute x3, waiting for transfers between devices, per_device(): near.append(lax.ppermute(other if k % 2 else same, 'seq', route))  4.8 us
    ppermute x3, starting transfers between devices, per_device(): near.append(lax.ppermute(other if k % 2 else same, 'seq', route))  4.18 us
    ppermute x3, waiting for transfers between devices, per_device(): all_query.append(lax.ppermute(near_query, 'seq', route))  3.89 us
    ppermute x1, waiting for transfers between devices, per_device(): table = lax.ppermute(block_table.reshape(1, -1), 'grp', swap)  2.08 us
  transfers between devices with their start and end apart: 9, of which 6 were waited for; matrix products, arithmetic and copies ran while one was open for 1% of the time, Pallas kernels for 2%

profile of v4, /device:TPU:32, one launch (start us, length us, event | category | flops | bytes accessed | tf_op | source)
XLA Modules:
  0.0 64.3 jit_solution(10431505345863655586)
XLA Ops:
  0.0 0.0 collective-permute-start.1
  0.0 0.5 collective-permute-start
  0.5 0.7 %broadcast_clamp_fusion.request_ref = s32[1,16]{1,0:T(1,128)S(1)} fusion(s32[1,16]{1,0:T(1,128)} %request_ref.1), kind=kLoop, calls=%fused_computation.4 | loop fusion | flops 16 | bytes 128 | tf_op jit(solution)/shard_map/jit(clip)/min | solution.py:228
  1.2 2.1 %collective-permute-done.table_ref = s32[1,16]{1,0:T(1,128)S(1)} collective-permute-done((s32[1,16]{1,0:T(1,128)}, s32[1,16]{1,0:T(1,128)S(1)}, u32[]{:S(2)}, u32[]{:S(2)}) %collective-permute-start) | collective-permute-done | bytes 96 | tf_op jit(solution)/shard_map/ppermute | solution.py:227
  3.2 0.0 collective-permute-done.1.pool_ref
  3.2 1.8 %pack.1 = bf16[16,32,1152]{2,1,0:T(8,128)(2,1)} custom-call(s32[1,16]{1,0:T(1,128)S(1)} %broadcast_clamp_fusion.request_ref, s32[1,16]{1,0:T(1,128)S(1)} %collective-permute-done.table_ref, bf16[16,64,576]{2,1,0:T(8,128)(2,1)S(1)} %collective-permute-done.1.pool_ref), custom_call_target="tpu_custom_call" | custom-call | tf_op jit(solution)/shard_map/pack/pallas_call | solution.py:230
  5.1 0.0 copy-start.1
  5.1 0.0 copy-start.2
  5.1 0.0 copy-start.3
  5.1 0.0 copy-start.4
  5.1 9.7 %all-to-all-start = ((bf16[16,32,1152]{2,1,0:T(8,128)(2,1)}), bf16[16,32,1152]{2,1,0:T(8,128)(2,1)S(1)}, u32[]{:S(2)}, u32[]{:S(2)}) async-start(bf16[16,32,1152]{2,1,0:T(8,128)(2,1)} %pack.1), calls=%async_computation | async-start | bytes 2359296 | tf_op jit(solution)/shard_map/all_to_all | solution.py:243
  14.9 0.0 copy-start.5
  14.9 0.1 pad_add_fusion.place_ref
  15.0 0.0 copy-done.1
  15.0 0.0 copy-done.2
  15.0 0.0 copy-done.3
  15.0 0.0 copy-done.4
  15.0 0.9 %query.1 = (bf16[2,32,640]{2,1,0:T(8,128)(2,1)S(1)}, f32[2,512]{1,0:T(2,128)S(1)}) custom-call(s32[3]{0:T(128)S(1)} %pad_add_fusion.place_ref, s32[2,16]{1,0:T(2,128)S(1)} %copy-done.3, s32[1,16]{1,0:T(1,128)S(1)} %copy-done.4, bf16[64,192]{1,0:T(8,128)(2,1)S(1)} %bitcast.13, bf16[8,128,512]{2,1,0:T(8,128)(2,1)S(1)} %copy-done.1), custom_call_target="tpu_custom_call" | custom-call | tf_op jit(solution)/shard_map/query/pallas_call | solution.py:248
  15.9 3.0 %collective-permute-start.4 = (bf16[32,640]{1,0:T(8,128)(2,1)S(1)}, bf16[32,640]{1,0:T(8,128)(2,1)S(1)}, u32[]{:S(2)}, u32[]{:S(2)}) collective-permute-start(bf16[32,640]{1,0:T(8,128)(2,1)S(1)} %get-tuple-element.30), channel_id=1, source_target_pairs={{0,24},{8,16},{16,8},{24,0},{32,56},{40,48},{48,40},{56,32},{64,88... | collective-permute-start | bytes 122888 | tf_op jit(solution)/shard_map/ppermute | solution.py:266
  18.9 0.6 collective-permute-start.3
  19.5 0.6 collective-permute-start.2
  20.1 1.1 %collective-permute-done.4 = bf16[32,640]{1,0:T(8,128)(2,1)S(1)} collective-permute-done((bf16[32,640]{1,0:T(8,128)(2,1)S(1)}, bf16[32,640]{1,0:T(8,128)(2,1)S(1)}, u32[]{:S(2)}, u32[]{:S(2)}) %collective-permute-start.4) | collective-permute-done | bytes 40992 | tf_op jit(solution)/shard_map/ppermute | solution.py:266
  21.2 3.7 %collective-permute-done.3 = bf16[32,640]{1,0:T(8,128)(2,1)S(1)} collective-permute-done((bf16[32,640]{1,0:T(8,128)(2,1)S(1)}, bf16[32,640]{1,0:T(8,128)(2,1)S(1)}, u32[]{:S(2)}, u32[]{:S(2)}) %collective-permute-start.3) | collective-permute-done | bytes 40992 | tf_op jit(solution)/shard_map/ppermute | solution.py:266
  24.9 0.0 collective-permute-done.2
  24.9 1.6 %collective-permute-start.5 = (bf16[128,640]{1,0:T(8,128)(2,1)S(1)}, bf16[128,640]{1,0:T(8,128)(2,1)S(1)}, u32[]{:S(2)}, u32[]{:S(2)}) collective-permute-start(bf16[128,640]{1,0:T(8,128)(2,1)S(1)} %pad_maximum_fusion.refs_0_), channel_id=1, source_target_pairs={{0,32},{8,40},{16,48},{24,56},{32,64},{40,72},{48,80},{56,88},{64,... | collective-permute-start | bytes 491528 | tf_op jit(solution)/shard_map/ppermute | solution.py:271
  26.5 2.7 %collective-permute-start.6 = (bf16[128,640]{1,0:T(8,128)(2,1)S(1)}, bf16[128,640]{1,0:T(8,128)(2,1)S(1)}, u32[]{:S(2)}, u32[]{:S(2)}) collective-permute-start(bf16[128,640]{1,0:T(8,128)(2,1)S(1)} %pad_maximum_fusion.refs_0_), channel_id=1, source_target_pairs={{0,64},{8,72},{16,80},{24,88},{32,96},{40,104},{48,112},{56,120},{... | collective-permute-start | bytes 491528 | tf_op jit(solution)/shard_map/ppermute | solution.py:271
  29.2 1.4 %collective-permute-start.7 = (bf16[128,640]{1,0:T(8,128)(2,1)S(1)}, bf16[128,640]{1,0:T(8,128)(2,1)S(1)}, u32[]{:S(2)}, u32[]{:S(2)}) collective-permute-start(bf16[128,640]{1,0:T(8,128)(2,1)S(1)} %pad_maximum_fusion.refs_0_), channel_id=1, source_target_pairs={{0,96},{8,104},{16,112},{24,120},{32,0},{40,8},{48,16},{56,24},{64... | collective-permute-start | bytes 491528 | tf_op jit(solution)/shard_map/ppermute | solution.py:271
  30.6 0.0 copy-done.5
  30.6 0.4 fresh.1
  31.0 2.1 %collective-permute-done.5.refs_1_ = bf16[128,640]{1,0:T(8,128)(2,1)S(1)} collective-permute-done((bf16[128,640]{1,0:T(8,128)(2,1)S(1)}, bf16[128,640]{1,0:T(8,128)(2,1)S(1)}, u32[]{:S(2)}, u32[]{:S(2)}) %collective-permute-start.5) | collective-permute-done | bytes 163872 | tf_op jit(solution)/shard_map/ppermute | solution.py:271
  33.2 1.8 %collective-permute-done.6.refs_2_ = bf16[128,640]{1,0:T(8,128)(2,1)S(1)} collective-permute-done((bf16[128,640]{1,0:T(8,128)(2,1)S(1)}, bf16[128,640]{1,0:T(8,128)(2,1)S(1)}, u32[]{:S(2)}, u32[]{:S(2)}) %collective-permute-start.6) | collective-permute-done | bytes 163872 | tf_op jit(solution)/shard_map/ppermute | solution.py:271
  34.9 0.0 collective-permute-done.7.refs_3_
  34.9 9.3 %all-to-all-done = bf16[16,32,1152]{2,1,0:T(8,128)(2,1)S(1)} async-done(((bf16[16,32,1152]{2,1,0:T(8,128)(2,1)}), bf16[16,32,1152]{2,1,0:T(8,128)(2,1)S(1)}, u32[]{:S(2)}, u32[]{:S(2)}) %all-to-all-start) | async-done | bytes 1179680 | tf_op jit(solution)/shard_map/all_to_all | solution.py:243
  44.2 0.0 copy-start
  44.2 1.9 %attend.1 = bf16[16,144,128]{2,1,0:T(8,128)(2,1)S(1)} custom-call(f32[2,512]{1,0:T(2,128)S(1)} %get-tuple-element.17.bias_ref, bf16[512,1152]{1,0:T(8,128)(2,1)S(1)} %bitcast.12, bf16[128,640]{1,0:T(8,128)(2,1)S(1)} %pad_maximum_fusion.refs_0_, bf16[128,640]{1,0:T(8,128)(2,1)S(1)} %collective-permute-done.5.refs_1_, ...), custom_call_target="tpu_custom_call" | custom-call | tf_op jit(solution)/shard_map/attend/pallas_call | solution.py:287
  46.1 17.0 %all_to_all.10.got_ref = bf16[16,144,128]{2,1,0:T(8,128)(2,1)S(1)} all-to-all(bf16[16,144,128]{2,1,0:T(8,128)(2,1)S(1)} %attend.1), channel_id=1, replica_groups=mesh['grp'=2,'seq'=16,'row'=8] {'seq'}, dimensions={0} | all-to-all | bytes 1179648 | tf_op jit(solution)/shard_map/all_to_all | solution.py:299
  63.2 0.0 copy-done
  63.2 1.2 %merge.1 = bf16[64,128]{1,0:T(8,128)(2,1)} custom-call(bf16[16,144,128]{2,1,0:T(8,128)(2,1)S(1)} %all_to_all.10.got_ref, f32[64,128]{1,0:T(8,128)S(1)} %get-tuple-element.26.best_ref, f32[64,128]{1,0:T(8,128)S(1)} %get-tuple-element.27.sum_ref, f32[64,512]{1,0:T(8,128)S(1)} %get-tuple-element.28.value_ref, bf16[8,512,128]{2,1,0:T(8,128)(2,1)S(1)} %copy-done), custom_call_target="tpu_custom_call" | custom-call | tf_op jit(solution)/shard_map/merge/pallas_call | solution.py:301
  (3 shorter events, 0.1 us)
Async XLA Ops:
  0.0 3.2 %collective-permute-start.1 = (bf16[16,64,576]{2,1,0:T(8,128)(2,1)}, bf16[16,64,576]{2,1,0:T(8,128)(2,1)S(1)}, u32[]{:S(2)}, u32[]{:S(2)}) collective-permute-start(bf16[16,64,576]{2,1,0:T(8,128)(2,1)} %bitcast.14), channel_id=1, source_target_pairs={{0,128},{128,0},{1,129},{129,1},{2,130},{130,2},{3,131},{131,3},{4... | collective-permute-start | bytes 3538952 | tf_op jit(solution)/shard_map/ppermute | solution.py:226
  0.0 3.2 %collective-permute-start = (s32[1,16]{1,0:T(1,128)}, s32[1,16]{1,0:T(1,128)S(1)}, u32[]{:S(2)}, u32[]{:S(2)}) collective-permute-start(s32[1,16]{1,0:T(1,128)} %bitcast.15), channel_id=1, source_target_pairs={{0,128},{128,0},{1,129},{129,1},{2,130},{130,2},{3,131},{131,3},{4... | collective-permute-start | bytes 200 | tf_op jit(solution)/shard_map/ppermute | solution.py:227
  5.1 9.9 %copy-start.1 = (bf16[8,128,512]{2,1,0:T(8,128)(2,1)S(1)}, bf16[8,128,512]{2,1,0:T(8,128)(2,1)}, u32[]{:S(2)}) copy-start(bf16[8,128,512]{2,1,0:T(8,128)(2,1)} %w_ref.2) | copy-start | bytes 3145732
  5.1 9.9 %copy-start.2 = (bf16[1,2,4,8,192]{4,3,2,1,0:T(8,128)(2,1)S(1)}, bf16[1,2,4,8,192]{4,3,2,1,0:T(8,128)(2,1)}, u32[]{:S(2)}) copy-start(bf16[1,2,4,8,192]{4,3,2,1,0:T(8,128)(2,1)} %param.12) | copy-start | bytes 73732
  5.1 9.9 %copy-start.3 = (s32[2,16]{1,0:T(2,128)S(1)}, s32[2,16]{1,0:T(2,128)}, u32[]{:S(2)}) copy-start(s32[2,16]{1,0:T(2,128)} %lengths_ref.1) | copy-start | bytes 388
  5.1 9.9 %copy-start.4 = (s32[1,16]{1,0:T(1,128)S(1)}, s32[1,16]{1,0:T(1,128)}, u32[]{:S(2)}) copy-start(s32[1,16]{1,0:T(1,128)} %request_ref.1) | copy-start | bytes 196
  5.1 39.1 %all-to-all-start = ((bf16[16,32,1152]{2,1,0:T(8,128)(2,1)}), bf16[16,32,1152]{2,1,0:T(8,128)(2,1)S(1)}, u32[]{:S(2)}, u32[]{:S(2)}) async-start(bf16[16,32,1152]{2,1,0:T(8,128)(2,1)} %pack.1), calls=%async_computation | async-start | bytes 2359296 | tf_op jit(solution)/shard_map/all_to_all | solution.py:243
  14.9 15.7 %copy-start.5 = (bf16[1,2,4,576]{3,2,1,0:T(4,128)(2,1)S(1)}, bf16[1,2,4,576]{3,2,1,0:T(4,128)(2,1)}, u32[]{:S(2)}) copy-start(bf16[1,2,4,576]{3,2,1,0:T(4,128)(2,1)} %param.13) | copy-start | bytes 27652
  15.9 5.3 %collective-permute-start.4 = (bf16[32,640]{1,0:T(8,128)(2,1)S(1)}, bf16[32,640]{1,0:T(8,128)(2,1)S(1)}, u32[]{:S(2)}, u32[]{:S(2)}) collective-permute-start(bf16[32,640]{1,0:T(8,128)(2,1)S(1)} %get-tuple-element.30), channel_id=1, source_target_pairs={{0,24},{8,16},{16,8},{24,0},{32,56},{40,48},{48,40},{56,32},{64,88... | collective-permute-start | bytes 122888 | tf_op jit(solution)/shard_map/ppermute | solution.py:266
  18.9 6.0 %collective-permute-start.3 = (bf16[32,640]{1,0:T(8,128)(2,1)S(1)}, bf16[32,640]{1,0:T(8,128)(2,1)S(1)}, u32[]{:S(2)}, u32[]{:S(2)}) collective-permute-start(bf16[32,640]{1,0:T(8,128)(2,1)S(1)} %get-tuple-element.29), channel_id=1, source_target_pairs={{0,16},{8,24},{16,0},{24,8},{32,48},{40,56},{48,32},{56,40},{64,80... | collective-permute-start | bytes 122888 | tf_op jit(solution)/shard_map/ppermute | solution.py:266
  19.5 5.4 %collective-permute-start.2 = (bf16[32,640]{1,0:T(8,128)(2,1)S(1)}, bf16[32,640]{1,0:T(8,128)(2,1)S(1)}, u32[]{:S(2)}, u32[]{:S(2)}) collective-permute-start(bf16[32,640]{1,0:T(8,128)(2,1)S(1)} %get-tuple-element.30), channel_id=1, source_target_pairs={{0,8},{8,0},{16,24},{24,16},{32,40},{40,32},{48,56},{56,48},{64,72... | collective-permute-start | bytes 122888 | tf_op jit(solution)/shard_map/ppermute | solution.py:266
  24.9 8.3 %collective-permute-start.5 = (bf16[128,640]{1,0:T(8,128)(2,1)S(1)}, bf16[128,640]{1,0:T(8,128)(2,1)S(1)}, u32[]{:S(2)}, u32[]{:S(2)}) collective-permute-start(bf16[128,640]{1,0:T(8,128)(2,1)S(1)} %pad_maximum_fusion.refs_0_), channel_id=1, source_target_pairs={{0,32},{8,40},{16,48},{24,56},{32,64},{40,72},{48,80},{56,88},{64,... | collective-permute-start | bytes 491528 | tf_op jit(solution)/shard_map/ppermute | solution.py:271
  26.5 8.5 %collective-permute-start.6 = (bf16[128,640]{1,0:T(8,128)(2,1)S(1)}, bf16[128,640]{1,0:T(8,128)(2,1)S(1)}, u32[]{:S(2)}, u32[]{:S(2)}) collective-permute-start(bf16[128,640]{1,0:T(8,128)(2,1)S(1)} %pad_maximum_fusion.refs_0_), channel_id=1, source_target_pairs={{0,64},{8,72},{16,80},{24,88},{32,96},{40,104},{48,112},{56,120},{... | collective-permute-start | bytes 491528 | tf_op jit(solution)/shard_map/ppermute | solution.py:271
  29.2 5.8 %collective-permute-start.7 = (bf16[128,640]{1,0:T(8,128)(2,1)S(1)}, bf16[128,640]{1,0:T(8,128)(2,1)S(1)}, u32[]{:S(2)}, u32[]{:S(2)}) collective-permute-start(bf16[128,640]{1,0:T(8,128)(2,1)S(1)} %pad_maximum_fusion.refs_0_), channel_id=1, source_target_pairs={{0,96},{8,104},{16,112},{24,120},{32,0},{40,8},{48,16},{56,24},{64... | collective-permute-start | bytes 491528 | tf_op jit(solution)/shard_map/ppermute | solution.py:271
  44.2 19.0 %copy-start = (bf16[8,512,128]{2,1,0:T(8,128)(2,1)S(1)}, bf16[8,512,128]{2,1,0:T(8,128)(2,1)}, u32[]{:S(2)}) copy-start(bf16[8,512,128]{2,1,0:T(8,128)(2,1)} %w_ref.3) | copy-start | bytes 3145732

commit v5 on v4

--- a/solution.py
+++ b/solution.py
@@ -7,7 +7,7 @@
 from jax.experimental.pallas import tpu as pltpu
 from jax.sharding import PartitionSpec as P
 
-FILL_LOW = -1e30
+FILL_LOW = -(2.0**100)
 LOG2_E = 1.4426950408889634
 LANES = 128
 FOLD = 16
@@ -28,11 +28,10 @@
     return pltpu.CompilerParams(vmem_limit_bytes=mib << 20)
 
 
-def pack_kernel(request_ref, table_ref, pool_ref, out_ref, packed, sems):
+def pack_kernel(request_ref, table_ref, pool_ref, packed):
     n_peer, half_page, _ = packed.shape
     latent = packed.shape[2] // 2 - LANES // 2
     n_row = n_peer // 2
-    stores = []
     for peer in range(n_peer):
         page = table_ref[0, request_ref[0, peer % n_row * 2 + peer // n_row]]
         packed[peer, :, :latent] = pool_ref[page, :half_page, :latent]
@@ -40,10 +39,6 @@
             [pool_ref[page, :half_page, latent:], pool_ref[page, half_page:, latent:]], axis=1
         )
         packed[peer, :, latent + LANES :] = pool_ref[page, half_page:, :latent]
-        stores.append(pltpu.make_async_copy(packed.at[peer], out_ref.at[peer], sems.at[peer]))
-        stores[peer].start()
-    for store in stores:
-        store.wait()
 
 
 def query_kernel(place_ref, lengths_ref, request_ref, query_ref, w_ref, out_ref, bias_ref):
@@ -53,11 +48,11 @@
     n_row = request_ref.shape[1] // 2
     keys = bias_ref.shape[1]
     half_page = keys // (2 * n_row)
-    pair = seq % 2
+    pair = seq // N_NEAR % 2
     length = lengths_ref[group, request_ref[0, row * 2 + pair]]
     key_id = lax.broadcasted_iota(jnp.int32, (1, keys), 1)
     source = key_id // half_page
-    block = (seq - pair + source // n_row) * n_row + source % n_row
+    block = (seq + (source // n_row - pair) * N_NEAR) * n_row + source % n_row
     for h in range(2):
         position = block * (2 * half_page) + h * half_page + key_id % half_page
         bias_ref[h : h + 1, :] = jnp.where(position < length, 0.0, FILL_LOW)
@@ -85,46 +80,60 @@
     return parts
 
 
-def attend_kernel(scale2, bias_ref, cache_ref, *refs):
-    query_refs, (out_ref, score_ref, weight_ref) = refs[:-3], refs[-3:]
+def side_kernel(*refs):
+    query_refs, side_ref = refs[:-1], refs[-1]
     seq = lax.axis_index("seq")
-    n_seq = out_ref.shape[0]
     n_far = len(query_refs)
     rows = query_refs[0].shape[0] // N_NEAR
+    latent = side_ref.shape[2] - LANES
+    low = lax.broadcasted_iota(jnp.int32, (rows, LANES), 1) < LANES // 2
+    near, far = seq // N_NEAR, seq % N_NEAR
+    for j in range(n_far):
+        for k in range(N_NEAR):
+            owner = (near ^ k) * N_NEAR + (far + n_far - j) % n_far
+            span = pl.ds(pl.multiple_of(owner * rows, rows), rows)
+            block = query_refs[j][k * rows : (k + 1) * rows, :]
+            plain, rope = block[:, :latent], block[:, latent:]
+            zero = jnp.zeros_like(rope)
+            side_ref[0, span, :latent] = plain
+            side_ref[0, span, latent:] = jnp.where(low, rope, zero)
+            side_ref[1, span, :LANES] = jnp.where(low, zero, rope)
+            side_ref[1, span, LANES:] = plain
+
+
+def pair_kernel(w_ref, out_ref):
+    width = w_ref.shape[2]
+    for h in range(w_ref.shape[0]):
+        out_ref[h // 2, :, h % 2 * width : (h % 2 + 1) * width] = w_ref[h]
+
+
+def attend_kernel(scale2, bias_ref, side_ref, cache_ref, out_ref, score_ref, weight_ref):
+    n_seq = out_ref.shape[0]
+    rows = side_ref.shape[1] // n_seq
     latent = (cache_ref.shape[1] - LANES) // 2
     chunks = latent // LANES
     lane = lax.broadcasted_iota(jnp.int32, (rows, LANES), 1)
     base = PARTS * (lax.broadcasted_iota(jnp.int32, (rows, LANES), 0) // FOLD)
-    far, near = seq // N_NEAR, seq % N_NEAR
-    owner = [
-        (far + n_far - b // N_NEAR) % n_far * N_NEAR + (near ^ (b % N_NEAR)) for b in range(n_seq)
-    ]
-    query = jnp.concatenate([ref[...] for ref in query_refs], axis=0)
-    plain, rope = query[:, :latent], query[:, latent:]
-    low = lax.broadcasted_iota(jnp.int32, rope.shape, 1) < LANES // 2
-    zero = jnp.zeros_like(rope)
     for h in range(2):
-        if h == 0:
-            side = jnp.concatenate([plain, jnp.where(low, rope, zero)], axis=1)
-        else:
-            side = jnp.concatenate([jnp.where(low, zero, rope), plain], axis=1)
         score_ref[h] = lax.dot_general(
-            side, cache_ref[:, h * latent : (h + 1) * latent + LANES], NT,
+            side_ref[h], cache_ref[:, h * latent : (h + 1) * latent + LANES], NT,
             preferred_element_type=jnp.float32,
         )
     for b in range(n_seq):
         block = slice(b * rows, (b + 1) * rows)
         scores = [score_ref[h, block] + bias_ref[h : h + 1, :] for h in range(2)]
         best = jnp.max(jnp.maximum(*scores), axis=1, keepdims=True)
+        best_parts = split_bf16(best, 2)
+        best = best_parts[0] + best_parts[1]
         weights = [jnp.exp2((one - best) * scale2) for one in scores]
         for h in range(2):
             weight_ref[h, block] = weights[h].astype(jnp.bfloat16)
         weight_sum = jnp.sum(weights[0] + weights[1], axis=1, keepdims=True)
         stats = jnp.zeros((rows, LANES), jnp.float32)
-        for j, part in enumerate(split_bf16(best * scale2, 3) + split_bf16(weight_sum, 2)):
+        for j, part in enumerate(best_parts + split_bf16(weight_sum, 2)):
             stats = jnp.where(lane == base + j, part, stats)
         stats = sum(stats[i * FOLD : (i + 1) * FOLD] for i in range(rows // FOLD))
-        out_ref[owner[b], chunks * rows :, :] = stats.astype(jnp.bfloat16)
+        out_ref[b, chunks * rows :, :] = stats.astype(jnp.bfloat16)
     value = jnp.dot(weight_ref[0], cache_ref[:, :latent], preferred_element_type=jnp.float32)
     value += jnp.dot(
         weight_ref[1], cache_ref[:, latent + LANES :], preferred_element_type=jnp.float32
@@ -132,7 +141,7 @@
     value = value.astype(jnp.bfloat16)
     for b in range(n_seq):
         for c in range(chunks):
-            out_ref[owner[b], c * rows : (c + 1) * rows, :] = (
+            out_ref[b, c * rows : (c + 1) * rows, :] = (
                 value[b * rows : (b + 1) * rows, c * LANES : (c + 1) * LANES]
             )
 
@@ -162,25 +171,26 @@
         value_ref[part] = value
 
 
-def merge_kernel(got_ref, best_ref, sum_ref, value_ref, w_ref, out_ref):
+def merge_kernel(scale2, got_ref, best_ref, sum_ref, value_ref, w_ref, out_ref):
     n_seq = got_ref.shape[0]
-    heads, latent, _ = w_ref.shape
+    heads, latent = 2 * w_ref.shape[0], w_ref.shape[1]
     rows = best_ref.shape[0] // 2
     chunks = latent // LANES
     tail = chunks * rows
     lane = lax.broadcasted_iota(jnp.int32, (rows, LANES), 1)
     base = PARTS * (lax.broadcasted_iota(jnp.int32, (rows, LANES), 0) // FOLD)
-    in_best = (lane >= base) & (lane < base + 3)
-    in_sum = (lane >= base + 3) & (lane < base + 5)
+    in_best = (lane >= base) & (lane < base + 2)
+    in_sum = (lane >= base + 2) & (lane < base + 4)
     latent_out = []
     for r in range(2):
         part = slice(r * rows, (r + 1) * rows)
-        sources = range(r, n_seq, 2)
+        sources = [i for i in range(n_seq) if i // N_NEAR % 2 == r]
         bests, sums = [], []
         for i in sources:
             stats = got_ref[i, tail:, :].astype(jnp.float32)
             stats = jnp.concatenate([stats] * (rows // FOLD), axis=0)
-            bests.append(jnp.sum(jnp.where(in_best, stats, 0.0), axis=1, keepdims=True))
+            best = jnp.sum(jnp.where(in_best, stats, 0.0), axis=1, keepdims=True)
+            bests.append(best * scale2)
             sums.append(jnp.sum(jnp.where(in_sum, stats, 0.0), axis=1, keepdims=True))
         fresh_best = best_ref[part]
         best = fresh_best
@@ -202,9 +212,11 @@
     latent_out = jnp.concatenate(latent_out, axis=0)
     head_of = lax.broadcasted_iota(jnp.int32, out_ref.shape, 0) % heads
     result = jnp.zeros(out_ref.shape, jnp.float32)
-    for h in range(heads):
-        one = jnp.dot(latent_out, w_ref[h], preferred_element_type=jnp.float32)
-        result = jnp.where(head_of == h, one, result)
+    width = out_ref.shape[1]
+    for p in range(heads // 2):
+        both = jnp.dot(latent_out, w_ref[p], preferred_element_type=jnp.float32)
+        result = jnp.where(head_of == 2 * p, both[:, :width], result)
+        result = jnp.where(head_of == 2 * p + 1, both[:, width:], result)
     out_ref[...] = result.astype(jnp.bfloat16)
 
 
@@ -231,14 +243,14 @@
         pack_kernel,
         out_shape=jax.ShapeDtypeStruct(packed_shape, bf16),
         in_specs=[smem(), smem(), vmem()],
-        out_specs=pl.BlockSpec(memory_space=pl.ANY),
-        scratch_shapes=[pltpu.VMEM(packed_shape, bf16), pltpu.SemaphoreType.DMA((2 * n_row,))],
-        compiler_params=params(16),
+        out_specs=vmem(),
+        compiler_params=params(8),
         name="pack",
     )(order, table, pool)
     pairs = [
-        [(base + pair) * n_row + row for pair in range(2) for row in range(n_row)]
-        for base in range(0, n_seq, 2)
+        [(base + pair * N_NEAR) * n_row + row for pair in range(2) for row in range(n_row)]
+        for base in range(n_seq)
+        if base // N_NEAR % 2 == 0
     ]
     got_cache = lax.all_to_all(
         packed, ("seq", "row"), 0, 0, axis_index_groups=pairs, tiled=True
@@ -256,18 +268,18 @@
         compiler_params=params(16),
         name="query",
     )(place, lengths, row_request, queries.reshape(block_rows, query_width), w_uk)
-    pair = lax.axis_index("seq") % 2
+    pair = lax.axis_index("seq") // N_NEAR % 2
     same, other = (
         lax.dynamic_index_in_dim(own_query, one, 0, keepdims=False) for one in (pair, 1 - pair)
     )
     near = [same]
     for k in range(1, N_NEAR):
-        route = [(s, s ^ k) for s in range(n_seq)]
+        route = [(s, s ^ (k * N_NEAR)) for s in range(n_seq)]
         near.append(lax.ppermute(other if k % 2 else same, "seq", route))
     near_query = jnp.concatenate(near, axis=0)
     all_query = [near_query]
     for j in range(1, n_seq // N_NEAR):
-        route = [(s, (s + j * N_NEAR) % n_seq) for s in range(n_seq)]
+        route = [(s, s // N_NEAR * N_NEAR + (s + j) % N_NEAR) for s in range(n_seq)]
         all_query.append(lax.ppermute(near_query, "seq", route))
 
     fresh = pl.pallas_call(
@@ -281,13 +293,29 @@
         compiler_params=params(16),
         name="fresh",
     )(own_query, new_latent.reshape(rows_dev * n_new, lat_width))
-    all_query, fresh = lax.optimization_barrier((all_query, fresh))
+    sides = pl.pallas_call(
+        side_kernel,
+        out_shape=jax.ShapeDtypeStruct((2, n_seq * half_rows, latent_dim + LANES), bf16),
+        in_specs=[vmem()] * len(all_query),
+        out_specs=vmem(),
+        compiler_params=params(16),
+        name="sides",
+    )(*all_query)
+    w_pairs = pl.pallas_call(
+        pair_kernel,
+        out_shape=jax.ShapeDtypeStruct((head_dev // 2, latent_dim, 2 * value_dim), bf16),
+        in_specs=[vmem()],
+        out_specs=vmem(),
+        compiler_params=params(16),
+        name="pairs",
+    )(w_uv)
+    sides, fresh, w_pairs = lax.optimization_barrier((sides, fresh, w_pairs))
 
     send_shape = (n_seq, half_rows * latent_dim // LANES + FOLD, LANES)
     message = pl.pallas_call(
         functools.partial(attend_kernel, scale2),
         out_shape=jax.ShapeDtypeStruct(send_shape, bf16),
-        in_specs=[vmem()] * (2 + len(all_query)),
+        in_specs=[vmem()] * 3,
         out_specs=vmem(),
         scratch_shapes=[
             pltpu.VMEM((2, n_seq * half_rows, keys), jnp.float32),
@@ -295,17 +323,17 @@
         ],
         compiler_params=params(32),
         name="attend",
-    )(bias, got_cache.reshape(keys, -1), *all_query)
+    )(bias, sides, got_cache.reshape(keys, -1))
     got = lax.all_to_all(message, "seq", 0, 0, tiled=True)
 
     result = pl.pallas_call(
-        merge_kernel,
+        functools.partial(merge_kernel, scale2),
         out_shape=jax.ShapeDtypeStruct((block_rows, value_dim), bf16),
         in_specs=[vmem()] * 5,
         out_specs=vmem(),
         compiler_params=params(16),
         name="merge",
-    )(got, *fresh, w_uv)
+    )(got, *fresh, w_pairs)
     return result.reshape(1, rows_dev, n_new, head_dev, value_dim)
 
 

time: 64.5 us -> 64.4 us (level)
  local copies, waits for them, and re-layouts: 0.07 us -> 7.57 us
  waiting for transfers between devices: 20 us -> 13.1 us
  starting transfers between devices: 20.2 us -> 19.1 us
    unnamed x12 -> x40, local copies, waits for them, and re-layouts: 0.03 us -> 7.53 us
    all_to_all x1, waiting for transfers between devices: 9.25 us -> 3.21 us  [per_device(): lax.all_to_all(packed, ('seq', 'row'), 0, 0, axis_index_groups=pairs, til...]
    ppermute x3, starting transfers between devices: 5.73 us -> 4.69 us  [per_device(): all_query.append(lax.ppermute(near_query, 'seq', route))]
    ppermute x3, waiting for transfers between devices: 4.8 us -> 4 us  [per_device(): near.append(lax.ppermute(other if k % 2 else same, 'seq', route))]
    pallas_call x1 -> x3, Pallas kernels: 1.16 us -> 1.4 us  [the longest x1 1.1 us: per_device(): pl.pallas_call(functools.partial(merge_kernel, scale2), out_shape=jax.Sha...]
  transfers between devices with their start and end apart: 9 -> 9, of which waited for: 6 -> 8; matrix products, arithmetic and copies ran while one was open for 1% -> 1% of each run, Pallas kernels for 2% -> 2%
where the time goes in v5:
time: 64.4 us; the launch traced here: 64 us
  starting transfers between devices  19.1 us (30%)
  blocking collectives  17 us (26%)
  waiting for transfers between devices  13.1 us (20%)
  local copies, waits for them, and re-layouts  7.57 us (12%)
  Pallas kernels  6.29 us (10%)
  other arithmetic  0.75 us (1%)
    all_to_all x1, blocking collectives, per_device(): got = lax.all_to_all(message, 'seq', 0, 0, tiled=True)  17 us
    all_to_all x1, starting transfers between devices, per_device(): lax.all_to_all(packed, ('seq', 'row'), 0, 0, axis_index_groups=pairs, til...  9.66 us
    unnamed x40, local copies, waits for them, and re-layouts  7.53 us
    ppermute x3, starting transfers between devices, per_device(): all_query.append(lax.ppermute(near_query, 'seq', route))  4.69 us
    ppermute x3, starting transfers between devices, per_device(): near.append(lax.ppermute(other if k % 2 else same, 'seq', route))  4.23 us
    ppermute x3, waiting for transfers between devices, per_device(): near.append(lax.ppermute(other if k % 2 else same, 'seq', route))  4 us
    ppermute x3, waiting for transfers between devices, per_device(): all_query.append(lax.ppermute(near_query, 'seq', route))  3.85 us
    all_to_all x1, waiting for transfers between devices, per_device(): lax.all_to_all(packed, ('seq', 'row'), 0, 0, axis_index_groups=pairs, til...  3.21 us
  transfers between devices with their start and end apart: 9, of which 8 were waited for; matrix products, arithmetic and copies ran while one was open for 1% of the time, Pallas kernels for 2%

profile of v5, /device:TPU:32, one launch (start us, length us, event | category | flops | bytes accessed | tf_op | source)
XLA Modules:
  0.0 64.0 jit_solution(2796925583256514279)
XLA Ops:
  0.0 0.0 collective-permute-start.7
  0.0 0.5 collective-permute-start.6
  0.5 0.7 %broadcast_clamp_fusion.request_ref = s32[1,16]{1,0:T(1,128)S(1)} fusion(s32[1,16]{1,0:T(1,128)} %request_ref.1), kind=kLoop, calls=%fused_computation.4 | loop fusion | flops 16 | bytes 128 | tf_op jit(solution)/shard_map/jit(clip)/min | solution.py:240
  1.2 2.1 %collective-permute-done.6.table_ref = s32[1,16]{1,0:T(1,128)S(1)} collective-permute-done((s32[1,16]{1,0:T(1,128)}, s32[1,16]{1,0:T(1,128)S(1)}, u32[]{:S(2)}, u32[]{:S(2)}) %collective-permute-start.6) | collective-permute-done | bytes 96 | tf_op jit(solution)/shard_map/ppermute | solution.py:239
  3.2 0.0 collective-permute-done.7.pool_ref
  3.2 1.7 %pack.1 = bf16[16,32,1152]{2,1,0:T(8,128)(2,1)} custom-call(s32[1,16]{1,0:T(1,128)S(1)} %broadcast_clamp_fusion.request_ref, s32[1,16]{1,0:T(1,128)S(1)} %collective-permute-done.6.table_ref, bf16[16,64,576]{2,1,0:T(8,128)(2,1)S(1)} %collective-permute-done.7.pool_ref), custom_call_target="tpu_custom_call" | custom-call | tf_op jit(solution)/shard_map/pack/pallas_call | solution.py:242
  5.0 9.7 %all-to-all-start = ((bf16[16,32,1152]{2,1,0:T(8,128)(2,1)}), bf16[16,32,1152]{2,1,0:T(8,128)(2,1)S(1)}, u32[]{:S(2)}, u32[]{:S(2)}) async-start(bf16[16,32,1152]{2,1,0:T(8,128)(2,1)} %pack.1), calls=%async_computation | async-start | bytes 2359296 | tf_op jit(solution)/shard_map/all_to_all | solution.py:255
  14.7 0.1 pad_add_fusion.place_ref
  14.8 0.0 copy-done
  14.8 0.0 copy-done.16
  14.8 0.0 copy-done.17
  14.8 0.0 copy-done.18
  14.8 0.9 %query.1 = (bf16[2,32,640]{2,1,0:T(8,128)(2,1)S(1)}, f32[2,512]{1,0:T(2,128)S(1)}) custom-call(s32[3]{0:T(128)S(1)} %pad_add_fusion.place_ref, s32[2,16]{1,0:T(2,128)S(1)} %copy-done.17, s32[1,16]{1,0:T(1,128)S(1)} %copy-done.18, bf16[64,192]{1,0:T(8,128)(2,1)S(1)} %bitcast.13, bf16[8,128,512]{2,1,0:T(8,128)(2,1)S(1)} %copy-done), custom_call_target="tpu_custom_call" | custom-call | tf_op jit(solution)/shard_map/query/pallas_call | solution.py:260
  15.7 2.8 %collective-permute-start.1 = (bf16[32,640]{1,0:T(8,128)(2,1)S(1)}, bf16[32,640]{1,0:T(8,128)(2,1)S(1)}, u32[]{:S(2)}, u32[]{:S(2)}) collective-permute-start(bf16[32,640]{1,0:T(8,128)(2,1)S(1)} %get-tuple-element.25), channel_id=1, source_target_pairs={{0,64},{8,72},{16,80},{24,88},{32,96},{40,104},{48,112},{56,120},{... | collective-permute-start | bytes 122888 | tf_op jit(solution)/shard_map/ppermute | solution.py:278
  18.5 1.4 %collective-permute-start.2 = (bf16[32,640]{1,0:T(8,128)(2,1)S(1)}, bf16[32,640]{1,0:T(8,128)(2,1)S(1)}, u32[]{:S(2)}, u32[]{:S(2)}) collective-permute-start(bf16[32,640]{1,0:T(8,128)(2,1)S(1)} %get-tuple-element.26), channel_id=1, source_target_pairs={{0,96},{8,104},{16,112},{24,120},{32,64},{40,72},{48,80},{56,88},{... | collective-permute-start | bytes 122888 | tf_op jit(solution)/shard_map/ppermute | solution.py:278
  19.9 0.0 collective-permute-start
  19.9 2.0 %collective-permute-done.1 = bf16[32,640]{1,0:T(8,128)(2,1)S(1)} collective-permute-done((bf16[32,640]{1,0:T(8,128)(2,1)S(1)}, bf16[32,640]{1,0:T(8,128)(2,1)S(1)}, u32[]{:S(2)}, u32[]{:S(2)}) %collective-permute-start.1) | collective-permute-done | bytes 40992 | tf_op jit(solution)/shard_map/ppermute | solution.py:278
  21.8 1.8 %collective-permute-done.2 = bf16[32,640]{1,0:T(8,128)(2,1)S(1)} collective-permute-done((bf16[32,640]{1,0:T(8,128)(2,1)S(1)}, bf16[32,640]{1,0:T(8,128)(2,1)S(1)}, u32[]{:S(2)}, u32[]{:S(2)}) %collective-permute-start.2) | collective-permute-done | bytes 40992 | tf_op jit(solution)/shard_map/ppermute | solution.py:278
  23.7 0.2 collective-permute-done
  23.9 0.0 copy-start.2
  23.9 3.1 %collective-permute-start.5 = (bf16[128,640]{1,0:T(8,128)(2,1)S(1)}, bf16[128,640]{1,0:T(8,128)(2,1)S(1)}, u32[]{:S(2)}, u32[]{:S(2)}) collective-permute-start(bf16[128,640]{1,0:T(8,128)(2,1)S(1)} %pad_maximum_fusion.refs_0_), channel_id=1, source_target_pairs={{0,24},{8,0},{16,8},{24,16},{32,56},{40,32},{48,40},{56,48},{64,88... | collective-permute-start | bytes 491528 | tf_op jit(solution)/shard_map/ppermute | solution.py:283
  27.0 0.6 collective-permute-start.4
  27.6 1.0 %collective-permute-start.3 = (bf16[128,640]{1,0:T(8,128)(2,1)S(1)}, bf16[128,640]{1,0:T(8,128)(2,1)S(1)}, u32[]{:S(2)}, u32[]{:S(2)}) collective-permute-start(bf16[128,640]{1,0:T(8,128)(2,1)S(1)} %pad_maximum_fusion.refs_0_), channel_id=1, source_target_pairs={{0,8},{8,16},{16,24},{24,0},{32,40},{40,48},{48,56},{56,32},{64,72... | collective-permute-start | bytes 491528 | tf_op jit(solution)/shard_map/ppermute | solution.py:283
  28.6 0.0 copy-done.19
  28.6 0.4 fresh.1
  29.0 0.0 copy-start.12
  29.0 0.6 copy-done.12
  29.6 1.2 %copy-done.1 = bf16[8,512,128]{2,1,0:T(8,128)(2,1)S(1)} copy-done((bf16[8,512,128]{2,1,0:T(8,128)(2,1)S(1)}, bf16[8,512,128]{2,1,0:T(8,128)(2,1)}, u32[]{:S(2)}) %copy-start.1) | copy-done | bytes 1048600
  30.9 0.2 pairs.1.w_ref
  31.1 1.5 %collective-permute-done.5.refs_3_ = bf16[128,640]{1,0:T(8,128)(2,1)S(1)} collective-permute-done((bf16[128,640]{1,0:T(8,128)(2,1)S(1)}, bf16[128,640]{1,0:T(8,128)(2,1)S(1)}, u32[]{:S(2)}, u32[]{:S(2)}) %collective-permute-start.5) | collective-permute-done | bytes 163872 | tf_op jit(solution)/shard_map/ppermute | solution.py:283
  32.6 0.7 %copy-done.4 = bf16[128,640]{1,0:T(8,128)(2,1)} copy-done((bf16[128,640]{1,0:T(8,128)(2,1)}, bf16[128,640]{1,0:T(8,128)(2,1)S(1)}, u32[]{:S(2)}) %copy-start.4) | copy-done | bytes 163864
  33.3 1.3 %collective-permute-done.4.refs_2_ = bf16[128,640]{1,0:T(8,128)(2,1)S(1)} collective-permute-done((bf16[128,640]{1,0:T(8,128)(2,1)S(1)}, bf16[128,640]{1,0:T(8,128)(2,1)S(1)}, u32[]{:S(2)}, u32[]{:S(2)}) %collective-permute-start.4) | collective-permute-done | bytes 163872 | tf_op jit(solution)/shard_map/ppermute | solution.py:283
  34.6 0.0 copy-done.2
  34.6 0.0 copy-done.10
  34.6 0.0 copy-start.6
  34.6 0.7 %copy-done.6 = bf16[128,640]{1,0:T(8,128)(2,1)} copy-done((bf16[128,640]{1,0:T(8,128)(2,1)}, bf16[128,640]{1,0:T(8,128)(2,1)S(1)}, u32[]{:S(2)}) %copy-start.6) | copy-done | bytes 163864
  35.3 1.0 %collective-permute-done.3.refs_1_ = bf16[128,640]{1,0:T(8,128)(2,1)S(1)} collective-permute-done((bf16[128,640]{1,0:T(8,128)(2,1)S(1)}, bf16[128,640]{1,0:T(8,128)(2,1)S(1)}, u32[]{:S(2)}, u32[]{:S(2)}) %collective-permute-start.3) | collective-permute-done | bytes 163872 | tf_op jit(solution)/shard_map/ppermute | solution.py:283
  36.3 0.7 %copy-done.8 = bf16[128,640]{1,0:T(8,128)(2,1)} copy-done((bf16[128,640]{1,0:T(8,128)(2,1)}, bf16[128,640]{1,0:T(8,128)(2,1)S(1)}, u32[]{:S(2)}) %copy-start.8) | copy-done | bytes 163864
  36.9 0.9 %copy-done.3 = bf16[128,640]{1,0:T(8,128)(2,1)S(1)} copy-done((bf16[128,640]{1,0:T(8,128)(2,1)S(1)}, bf16[128,640]{1,0:T(8,128)(2,1)}, u32[]{:S(2)}) %copy-start.3) | copy-done | bytes 163864
  37.9 0.9 %copy-done.5 = bf16[128,640]{1,0:T(8,128)(2,1)S(1)} copy-done((bf16[128,640]{1,0:T(8,128)(2,1)S(1)}, bf16[128,640]{1,0:T(8,128)(2,1)}, u32[]{:S(2)}) %copy-start.5) | copy-done | bytes 163864
  38.8 0.9 %copy-done.7 = bf16[128,640]{1,0:T(8,128)(2,1)S(1)} copy-done((bf16[128,640]{1,0:T(8,128)(2,1)S(1)}, bf16[128,640]{1,0:T(8,128)(2,1)}, u32[]{:S(2)}) %copy-start.7) | copy-done | bytes 163864
  39.7 0.9 %copy-done.9 = bf16[128,640]{1,0:T(8,128)(2,1)S(1)} copy-done((bf16[128,640]{1,0:T(8,128)(2,1)S(1)}, bf16[128,640]{1,0:T(8,128)(2,1)}, u32[]{:S(2)}) %copy-start.9) | copy-done | bytes 163864
  40.6 0.1 sides.1.side_ref
  40.7 3.2 %all-to-all-done = bf16[16,32,1152]{2,1,0:T(8,128)(2,1)S(1)} async-done(((bf16[16,32,1152]{2,1,0:T(8,128)(2,1)}), bf16[16,32,1152]{2,1,0:T(8,128)(2,1)S(1)}, u32[]{:S(2)}, u32[]{:S(2)}) %all-to-all-start) | async-done | bytes 1179680 | tf_op jit(solution)/shard_map/all_to_all | solution.py:255
  44.0 1.9 %attend.1 = bf16[16,144,128]{2,1,0:T(8,128)(2,1)S(1)} custom-call(f32[2,512]{1,0:T(2,128)S(1)} %get-tuple-element.15.bias_ref, bf16[2,512,640]{2,1,0:T(8,128)(2,1)S(1)} %sides.1.side_ref, bf16[512,1152]{1,0:T(8,128)(2,1)S(1)} %bitcast.12), custom_call_target="tpu_custom_call" | custom-call | tf_op jit(solution)/shard_map/attend/pallas_call | solution.py:315
  45.9 17.0 %all_to_all.10.got_ref = bf16[16,144,128]{2,1,0:T(8,128)(2,1)S(1)} all-to-all(bf16[16,144,128]{2,1,0:T(8,128)(2,1)S(1)} %attend.1), channel_id=1, replica_groups=mesh['grp'=2,'seq'=16,'row'=8] {'seq'}, dimensions={0} | all-to-all | bytes 1179648 | tf_op jit(solution)/shard_map/all_to_all | solution.py:327
  62.9 0.0 copy-done.11
  62.9 1.1 %merge.1 = bf16[64,128]{1,0:T(8,128)(2,1)} custom-call(bf16[16,144,128]{2,1,0:T(8,128)(2,1)S(1)} %all_to_all.10.got_ref, f32[64,128]{1,0:T(8,128)S(1)} %copy-done.13, f32[64,128]{1,0:T(8,128)S(1)} %copy-done.15, f32[64,512]{1,0:T(8,128)S(1)} %copy-done.11, bf16[4,512,256]{2,1,0:T(8,128)(2,1)S(1)} %pairs.1.w_ref), custom_call_target="tpu_custom_call" | custom-call | tf_op jit(solution)/shard_map/merge/pallas_call | solution.py:329
  (23 shorter events, 0.1 us)
Async XLA Ops:
  0.0 3.2 %collective-permute-start.7 = (bf16[16,64,576]{2,1,0:T(8,128)(2,1)}, bf16[16,64,576]{2,1,0:T(8,128)(2,1)S(1)}, u32[]{:S(2)}, u32[]{:S(2)}) collective-permute-start(bf16[16,64,576]{2,1,0:T(8,128)(2,1)} %bitcast.14), channel_id=1, source_target_pairs={{0,128},{128,0},{1,129},{129,1},{2,130},{130,2},{3,131},{131,3},{4... | collective-permute-start | bytes 3538952 | tf_op jit(solution)/shard_map/ppermute | solution.py:238
  0.0 3.2 %collective-permute-start.6 = (s32[1,16]{1,0:T(1,128)}, s32[1,16]{1,0:T(1,128)S(1)}, u32[]{:S(2)}, u32[]{:S(2)}) collective-permute-start(s32[1,16]{1,0:T(1,128)} %bitcast.15), channel_id=1, source_target_pairs={{0,128},{128,0},{1,129},{129,1},{2,130},{130,2},{3,131},{131,3},{4... | collective-permute-start | bytes 200 | tf_op jit(solution)/shard_map/ppermute | solution.py:239
  5.0 9.8 %copy-start = (bf16[8,128,512]{2,1,0:T(8,128)(2,1)S(1)}, bf16[8,128,512]{2,1,0:T(8,128)(2,1)}, u32[]{:S(2)}) copy-start(bf16[8,128,512]{2,1,0:T(8,128)(2,1)} %w_ref.2) | copy-start | bytes 3145732
  5.0 9.8 %copy-start.16 = (bf16[1,2,4,8,192]{4,3,2,1,0:T(8,128)(2,1)S(1)}, bf16[1,2,4,8,192]{4,3,2,1,0:T(8,128)(2,1)}, u32[]{:S(2)}) copy-start(bf16[1,2,4,8,192]{4,3,2,1,0:T(8,128)(2,1)} %param.12) | copy-start | bytes 73732
  5.0 9.8 %copy-start.17 = (s32[2,16]{1,0:T(2,128)S(1)}, s32[2,16]{1,0:T(2,128)}, u32[]{:S(2)}) copy-start(s32[2,16]{1,0:T(2,128)} %lengths_ref.1) | copy-start | bytes 388
  5.0 9.8 %copy-start.18 = (s32[1,16]{1,0:T(1,128)S(1)}, s32[1,16]{1,0:T(1,128)}, u32[]{:S(2)}) copy-start(s32[1,16]{1,0:T(1,128)} %request_ref.1) | copy-start | bytes 196
  5.0 39.0 %all-to-all-start = ((bf16[16,32,1152]{2,1,0:T(8,128)(2,1)}), bf16[16,32,1152]{2,1,0:T(8,128)(2,1)S(1)}, u32[]{:S(2)}, u32[]{:S(2)}) async-start(bf16[16,32,1152]{2,1,0:T(8,128)(2,1)} %pack.1), calls=%async_computation | async-start | bytes 2359296 | tf_op jit(solution)/shard_map/all_to_all | solution.py:255
  14.6 14.0 %copy-start.19 = (bf16[1,2,4,576]{3,2,1,0:T(4,128)(2,1)S(1)}, bf16[1,2,4,576]{3,2,1,0:T(4,128)(2,1)}, u32[]{:S(2)}) copy-start(bf16[1,2,4,576]{3,2,1,0:T(4,128)(2,1)} %param.13) | copy-start | bytes 27652
  15.7 6.2 %collective-permute-start.1 = (bf16[32,640]{1,0:T(8,128)(2,1)S(1)}, bf16[32,640]{1,0:T(8,128)(2,1)S(1)}, u32[]{:S(2)}, u32[]{:S(2)}) collective-permute-start(bf16[32,640]{1,0:T(8,128)(2,1)S(1)} %get-tuple-element.25), channel_id=1, source_target_pairs={{0,64},{8,72},{16,80},{24,88},{32,96},{40,104},{48,112},{56,120},{... | collective-permute-start | bytes 122888 | tf_op jit(solution)/shard_map/ppermute | solution.py:278
  18.5 5.2 %collective-permute-start.2 = (bf16[32,640]{1,0:T(8,128)(2,1)S(1)}, bf16[32,640]{1,0:T(8,128)(2,1)S(1)}, u32[]{:S(2)}, u32[]{:S(2)}) collective-permute-start(bf16[32,640]{1,0:T(8,128)(2,1)S(1)} %get-tuple-element.26), channel_id=1, source_target_pairs={{0,96},{8,104},{16,112},{24,120},{32,64},{40,72},{48,80},{56,88},{... | collective-permute-start | bytes 122888 | tf_op jit(solution)/shard_map/ppermute | solution.py:278
  19.9 4.0 %collective-permute-start = (bf16[32,640]{1,0:T(8,128)(2,1)S(1)}, bf16[32,640]{1,0:T(8,128)(2,1)S(1)}, u32[]{:S(2)}, u32[]{:S(2)}) collective-permute-start(bf16[32,640]{1,0:T(8,128)(2,1)S(1)} %get-tuple-element.26), channel_id=1, source_target_pairs={{0,32},{8,40},{16,48},{24,56},{32,0},{40,8},{48,16},{56,24},{64,96... | collective-permute-start | bytes 122888 | tf_op jit(solution)/shard_map/ppermute | solution.py:278
  23.9 10.7 %copy-start.2 = (bf16[128,640]{1,0:T(8,128)(2,1)}, bf16[128,640]{1,0:T(8,128)(2,1)S(1)}, u32[]{:S(2)}) copy-start(bf16[128,640]{1,0:T(8,128)(2,1)S(1)} %pad_maximum_fusion.refs_0_) | copy-start | bytes 491524
  23.9 8.7 %collective-permute-start.5 = (bf16[128,640]{1,0:T(8,128)(2,1)S(1)}, bf16[128,640]{1,0:T(8,128)(2,1)S(1)}, u32[]{:S(2)}, u32[]{:S(2)}) collective-permute-start(bf16[128,640]{1,0:T(8,128)(2,1)S(1)} %pad_maximum_fusion.refs_0_), channel_id=1, source_target_pairs={{0,24},{8,0},{16,8},{24,16},{32,56},{40,32},{48,40},{56,48},{64,88... | collective-permute-start | bytes 491528 | tf_op jit(solution)/shard_map/ppermute | solution.py:283
  27.0 7.6 %collective-permute-start.4 = (bf16[128,640]{1,0:T(8,128)(2,1)S(1)}, bf16[128,640]{1,0:T(8,128)(2,1)S(1)}, u32[]{:S(2)}, u32[]{:S(2)}) collective-permute-start(bf16[128,640]{1,0:T(8,128)(2,1)S(1)} %pad_maximum_fusion.refs_0_), channel_id=1, source_target_pairs={{0,16},{8,24},{16,0},{24,8},{32,48},{40,56},{48,32},{56,40},{64,80... | collective-permute-start | bytes 491528 | tf_op jit(solution)/shard_map/ppermute | solution.py:283
  27.6 8.6 %collective-permute-start.3 = (bf16[128,640]{1,0:T(8,128)(2,1)S(1)}, bf16[128,640]{1,0:T(8,128)(2,1)S(1)}, u32[]{:S(2)}, u32[]{:S(2)}) collective-permute-start(bf16[128,640]{1,0:T(8,128)(2,1)S(1)} %pad_maximum_fusion.refs_0_), channel_id=1, source_target_pairs={{0,8},{8,16},{16,24},{24,0},{32,40},{40,48},{48,56},{56,32},{64,72... | collective-permute-start | bytes 491528 | tf_op jit(solution)/shard_map/ppermute | solution.py:283
  29.0 0.6 copy-start.12
  29.6 1.2 %copy-start.1 = (bf16[8,512,128]{2,1,0:T(8,128)(2,1)S(1)}, bf16[8,512,128]{2,1,0:T(8,128)(2,1)}, u32[]{:S(2)}) copy-start(bf16[8,512,128]{2,1,0:T(8,128)(2,1)} %w_ref.3) | copy-start | bytes 3145732
  30.9 3.7 %copy-start.10 = (f32[64,512]{1,0:T(8,128)}, f32[64,512]{1,0:T(8,128)S(1)}, u32[]{:S(2)}) copy-start(f32[64,512]{1,0:T(8,128)S(1)} %get-tuple-element.23.value_ref) | copy-start | bytes 393220
  30.9 3.7 %copy-start.14 = (f32[64,128]{1,0:T(8,128)}, f32[64,128]{1,0:T(8,128)S(1)}, u32[]{:S(2)}) copy-start(f32[64,128]{1,0:T(8,128)S(1)} %get-tuple-element.22.sum_ref) | copy-start | bytes 98308
  32.6 0.7 %copy-start.4 = (bf16[128,640]{1,0:T(8,128)(2,1)}, bf16[128,640]{1,0:T(8,128)(2,1)S(1)}, u32[]{:S(2)}) copy-start(bf16[128,640]{1,0:T(8,128)(2,1)S(1)} %collective-permute-done.5.refs_3_) | copy-start | bytes 491524
  34.6 0.7 %copy-start.6 = (bf16[128,640]{1,0:T(8,128)(2,1)}, bf16[128,640]{1,0:T(8,128)(2,1)S(1)}, u32[]{:S(2)}) copy-start(bf16[128,640]{1,0:T(8,128)(2,1)S(1)} %collective-permute-done.4.refs_2_) | copy-start | bytes 491524
  36.3 0.7 %copy-start.8 = (bf16[128,640]{1,0:T(8,128)(2,1)}, bf16[128,640]{1,0:T(8,128)(2,1)S(1)}, u32[]{:S(2)}) copy-start(bf16[128,640]{1,0:T(8,128)(2,1)S(1)} %collective-permute-done.3.refs_1_) | copy-start | bytes 491524
  36.9 0.9 %copy-start.3 = (bf16[128,640]{1,0:T(8,128)(2,1)S(1)}, bf16[128,640]{1,0:T(8,128)(2,1)}, u32[]{:S(2)}) copy-start(bf16[128,640]{1,0:T(8,128)(2,1)} %copy-done.2) | copy-start | bytes 491524
  37.9 0.9 %copy-start.5 = (bf16[128,640]{1,0:T(8,128)(2,1)S(1)}, bf16[128,640]{1,0:T(8,128)(2,1)}, u32[]{:S(2)}) copy-start(bf16[128,640]{1,0:T(8,128)(2,1)} %copy-done.4) | copy-start | bytes 491524
  38.8 0.9 %copy-start.7 = (bf16[128,640]{1,0:T(8,128)(2,1)S(1)}, bf16[128,640]{1,0:T(8,128)(2,1)}, u32[]{:S(2)}) copy-start(bf16[128,640]{1,0:T(8,128)(2,1)} %copy-done.6) | copy-start | bytes 491524
  39.7 0.9 %copy-start.9 = (bf16[128,640]{1,0:T(8,128)(2,1)S(1)}, bf16[128,640]{1,0:T(8,128)(2,1)}, u32[]{:S(2)}) copy-start(bf16[128,640]{1,0:T(8,128)(2,1)} %copy-done.8) | copy-start | bytes 491524
  43.9 19.0 %copy-start.11 = (f32[64,512]{1,0:T(8,128)S(1)}, f32[64,512]{1,0:T(8,128)}, u32[]{:S(2)}) copy-start(f32[64,512]{1,0:T(8,128)} %copy-done.10) | copy-start | bytes 393220
  43.9 19.0 %copy-start.13 = (f32[64,128]{1,0:T(8,128)S(1)}, f32[64,128]{1,0:T(8,128)}, u32[]{:S(2)}) copy-start(f32[64,128]{1,0:T(8,128)} %copy-done.12) | copy-start | bytes 98308
  44.0 19.0 %copy-start.15 = (f32[64,128]{1,0:T(8,128)S(1)}, f32[64,128]{1,0:T(8,128)}, u32[]{:S(2)}) copy-start(f32[64,128]{1,0:T(8,128)} %copy-done.14) | copy-start | bytes 98308
